TPU v7x, 32 devices: a whole 2x2x4 slice. The times are simulated.
32 devices in a mesh: treated: 4 (over y, x), control: 8 (over z, core).
Axes of the slice: x: 2, y: 2, z: 4, core: 2. Of those that a mesh axis runs over, the one named last changes fastest.
Arguments:
- treated_emb: bfloat16 [4096, 1024], P(('treated', 'control')), may hold values from -20 to 20
- control_emb: bfloat16 [16384, 1024], P('control'), may hold values from -20 to 20
- control_pot: float32 [16384], P('control'), may hold values from -6 to 6
- control_logw: float32 [16384], P('control'), may hold values from -1.5 to 1.5
- treated_logw: float32 [4096], P('treated'), may hold values from -1.5 to 1.5
Outputs:
- treated_pot: float32 [4096], P('treated')
- column_lse: float32 [16384], P('control')
All inputs are finite; a program needn't handle non-finite values.
Results may differ from a plain program's by a relative error of at most 0.0003.
Values may be sent and summed in bfloat16 or wider, within the bound.
No kernel may reach another device: no remote copies, remote signals or barrier semaphores. Data moves between devices by JAX's collectives and lax.ppermute only.
A program may use at most 64 MiB of HBM per device.

v0:
```python
import jax
import jax.numpy as jnp
from jax import lax
from jax.sharding import PartitionSpec as P

smoothing = 0.1


def combined_all(part, axis, combine):
    gathered = jax.tree.map(lambda a: lax.all_gather(a, axis), part)

    def take(source):
        return jax.tree.map(lambda a: lax.dynamic_index_in_dim(a, source, 0, False), gathered)

    return lax.fori_loop(
        1, lax.axis_size(axis), lambda source, state: combine(state, take(source)), take(0)
    )


def merge_pairs(first, second):
    highest = jnp.maximum(first[0], second[0])
    total = first[1] * jnp.exp(first[0] - highest) + second[1] * jnp.exp(second[0] - highest)
    return (highest, total)


def body(treated_emb, control_emb, control_pot, control_logw, treated_logw):
    width = control_emb.shape[1]
    control_sq = jnp.sum(jnp.square(control_emb.astype(jnp.float32)), axis=1)
    column_bias = control_pot + control_logw
    slab_block = lax.all_gather(treated_emb, "control", axis=0, tiled=True)
    piece_sq = jnp.sum(jnp.square(slab_block.astype(jnp.float32)), axis=1)
    cross = lax.dot_general(
        slab_block, control_emb, (((1,), (1,)), ((), ())), preferred_element_type=jnp.float32
    )
    scaled = (piece_sq[:, None] + control_sq[None, :] - 2.0 * cross) / (width * smoothing)
    row_scores = column_bias[None, :] - scaled
    highest = lax.pmax(jnp.max(row_scores, axis=1), "control")
    total = lax.psum(jnp.sum(jnp.exp(row_scores - highest[:, None]), axis=1), "control")
    treated_pot = -(highest + jnp.log(total))
    column_scores = (treated_pot + treated_logw)[:, None] - scaled
    column_top = jnp.max(column_scores, axis=0)
    column_total = jnp.sum(jnp.exp(column_scores - column_top[None, :]), axis=0)
    summit, gathered_total = combined_all((column_top, column_total), "treated", merge_pairs)
    column_lse = summit + jnp.log(gathered_total)
    return (treated_pot, column_lse)


def solution(mesh):
    placed = (
        P(("treated", "control"), None),
        P("control", None),
        P("control"),
        P("control"),
        P("treated"),
    )
    return jax.shard_map(
        body, mesh=mesh, in_specs=placed, out_specs=(P("treated"), P("control")), check_vma=False
    )
```

profile of v0, /device:TPU:0, one launch (start us, length us, event | category | flops | bytes accessed | tf_op | source)
XLA Modules:
  0.0 120.8 jit_solution(11482562215332909332)
XLA Ops:
  7.2 0.0 all-gather.4.cloned.1.call-start
  7.2 0.7 all-gather.4.cloned.1.call-update
  7.9 0.7 add.74
  8.6 3.1 %multiply_reduce_fusion = f32[2048]{0:T(1024)S(1)} fusion(bf16[2048,1024]{1,0:T(8,128)(2,1)} %param.8), kind=kLoop, calls=%fused_computation.6 | loop fusion | flops 6289408 | bytes 4202496 | tf_op jit(solution)/shard_map/reduce_sum | solution.py:28
  11.7 29.7 %all-gather.4.cloned.1.call-done = bf16[1024,1024]{1,0:T(8,128)(2,1)} async-done(((bf16[128,1024]{1,0:T(8,128)(2,1)}), bf16[1024,1024]{1,0:T(8,128)(2,1)}) %all-gather.4.cloned.1.call-update) | async-done | bytes 2097168 | tf_op jit(solution)/shard_map/all_gather | solution.py:30
  41.4 2.1 %multiply_reduce_fusion.1 = f32[1024]{0:T(1024)S(1)} fusion(bf16[1024,1024]{1,0:T(8,128)(2,1)} %all-gather.4.cloned.1.call-done), kind=kLoop, calls=%fused_computation.9 | loop fusion | flops 3144704 | bytes 2101248 | tf_op jit(solution)/shard_map/reduce_sum | solution.py:31
  43.5 11.0 %subtract_reduce_fusion.1 = (f32[1024]{0:T(1024)S(1)}, f32[1024,2048]{1,0:T(8,128)}) fusion(f32[2048]{0:T(1024)S(1)} %add.74, bf16[1024,1024]{1,0:T(8,128)(2,1)} %all-gather.4.cloned.1.call-done, bf16[2048,1024]{1,0:T(8,128)(2,1)} %param.8, f32[2048]{0:T(1024)S(1)} %multiply_reduce_fusion, f32[1024]{0:T(1024)S(1)} %multiply_reduce_fusion.1), kind=kOutput, calls=%fused_computation.8 | convolution fusion | flops 4307549184 | bytes 14704640 | tf_op jit(solution)/shard_map/dot_general | solution.py:32
  54.5 0.0 copy-start
  54.5 15.5 %pmax.7 = f32[1024]{0:T(1024)S(1)} all-reduce(f32[1024]{0:T(1024)S(1)} %get-tuple-element.153), channel_id=1, replica_groups=mesh['treated'=4,'control'=8] {'control'}, use_global_device_ids=true, to_apply=%region_3.0 | all-reduce | flops 1024 | bytes 8192 | tf_op jit(solution)/shard_map/pmax | solution.py:37
  70.0 4.4 %exponential_reduce_fusion.1 = f32[1024]{0:T(1024)S(1)} fusion(f32[1024,2048]{1,0:T(8,128)} %get-tuple-element.154, f32[1024]{0:T(1024)S(1)} %pmax.7, f32[2048]{0:T(1024)S(1)} %add.74), kind=kLoop, calls=%fused_computation.4 | loop fusion | flops 6290432 | bytes 8404992 | tf_op jit(solution)/shard_map/reduce_sum | solution.py:38
  74.3 13.6 %psum.7 = f32[1024]{0:T(1024)S(1)} all-reduce(f32[1024]{0:T(1024)S(1)} %exponential_reduce_fusion.1), channel_id=1, replica_groups=mesh['treated'=4,'control'=8] {'control'}, use_global_device_ids=true, to_apply=%region_5.0 | all-reduce | flops 1024 | bytes 8192 | tf_op jit(solution)/shard_map/psum | solution.py:38
  87.9 0.0 copy-done
  87.9 0.6 fusion
  88.5 4.0 %subtract_reduce_fusion = f32[2048]{0:T(1024)S(1)} fusion(f32[1024,2048]{1,0:T(8,128)} %get-tuple-element.154, f32[1024]{0:T(1024)S(1)} %get-tuple-element.149), kind=kLoop, calls=%fused_computation.7 | loop fusion | flops 4192256 | bytes 8400896 | tf_op jit(solution)/shard_map/reduce_max | solution.py:41
  92.6 4.3 %exponential_reduce_fusion = f32[2048]{0:T(1024)S(1)} fusion(f32[1024,2048]{1,0:T(8,128)} %get-tuple-element.154, f32[2048]{0:T(1024)S(1)} %subtract_reduce_fusion, f32[1024]{0:T(1024)S(1)} %get-tuple-element.149), kind=kLoop, calls=%fused_computation.3 | loop fusion | flops 6289408 | bytes 8409088 | tf_op jit(solution)/shard_map/reduce_sum | solution.py:42
  96.9 8.1 %all-gather.1 = f32[8192]{0:T(1024)S(1)} all-gather(f32[2048]{0:T(1024)S(1)} %exponential_reduce_fusion), channel_id=3, replica_groups=mesh['treated'=4,'control'=8] {'treated'}, dimensions={0}, use_global_device_ids=true | all-gather | bytes 40960 | tf_op jit(solution)/shard_map/all_gather | solution.py:10
  105.0 8.1 %all-gather = f32[8192]{0:T(1024)S(1)} all-gather(f32[2048]{0:T(1024)S(1)} %subtract_reduce_fusion), channel_id=2, replica_groups=mesh['treated'=4,'control'=8] {'treated'}, dimensions={0}, use_global_device_ids=true | all-gather | bytes 40960 | tf_op jit(solution)/shard_map/all_gather | solution.py:10
  113.1 0.2 while.17
  113.3 0.6 log_add_fusion
  (10 shorter events, 0.1 us)
Async XLA Ops:
  7.2 34.3 %all-gather.4.cloned.1.call-start = ((), (), s32[]{:S(2)}) async-start(), calls=%async_computation | async-start | bytes 2359296 | tf_op jit(solution)/shard_map/all_gather | solution.py:30
  54.5 33.5 %copy-start = (f32[1024]{0:T(1024)S(1)}, f32[1024]{0:T(1024)}, u32[]{:S(2)}) copy-start(f32[1024]{0:T(1024)} %param.11) | copy-start | bytes 12292
Sparse Core Ops, SparseCore 0:
  9.6 31.7 all-gather.3
where the time goes:
time: 121 us
  blocking collectives  45.3 us (37%)
  waiting for transfers between devices  30.4 us (25%)
  other arithmetic  19.8 us (16%)
  between operations  14.1 us (12%)
  matrix products  11 us (9%)
    all_gather x1, waiting for transfers between devices, body(): slab_block = lax.all_gather(treated_emb, 'control', axis=0, tiled=True)  29.7 us
    all_gather x2, blocking collectives, combined_all(): gathered = jax.tree.map(lambda a: lax.all_gather(a, axis), part)  16.2 us
    pmax x1, blocking collectives, body(): highest = lax.pmax(jnp.max(row_scores, axis=1), 'control')  15.5 us
    psum x1, blocking collectives, body(): lax.psum(jnp.sum(jnp.exp(row_scores - highest[:, None]), axis=1), 'control')  13.6 us
    dot_general x1, matrix products, body(): lax.dot_general(slab_block, control_emb, (((1,), (1,)), ((), ())), prefer...  11 us
    reduce_sum x1, other arithmetic, body(): jnp.sum(jnp.exp(row_scores - highest[:, None]), axis=1)  4.37 us
    reduce_sum x1, other arithmetic, body(): column_total = jnp.sum(jnp.exp(column_scores - column_top[None, :]), axis=0)  4.3 us
    reduce_max x1, other arithmetic, body(): column_top = jnp.max(column_scores, axis=0)  4 us
  transfers between devices with their start and end apart: 1, of which 1 were waited for; matrix products, arithmetic and copies ran while one was open for 3% of the time, Pallas kernels for 0%

commit v1 on v0

v1 whole, which is shorter than its diff:
```python
import functools

import jax
import jax.numpy as jnp
from jax import lax
from jax.experimental import pallas as pl
from jax.experimental.pallas import tpu as pltpu
from jax.sharding import PartitionSpec as P

smoothing = 0.1
LOG2E = 1.4426950408889634
LN2 = 0.6931471805599453
LARGE = 2.0**30
SMALL = 2.0**-50
MIB = 1024 * 1024
NT_DIMS = (((1,), (1,)), ((), ()))
WHOLE = pl.BlockSpec(memory_space=pltpu.VMEM)


def params(limit):
    return pltpu.CompilerParams(vmem_limit_bytes=limit * MIB)


def canonical(held, piece):
    if held is None:
        return piece
    chips, places = held
    me = lax.axis_index("control")
    shift, flip = places[piece]
    return (me // 2 + chips - shift) % chips * 2 + (me % 2 + flip) % 2


def log2_sum(parts):
    top = functools.reduce(jnp.maximum, parts)
    return top + jnp.log2(functools.reduce(jnp.add, [jnp.exp2(p - top) for p in parts]))


def turned(column):
    return jnp.transpose(jnp.broadcast_to(column, (128, 128)))[0:1, :]


def tree_sum(parts):
    while len(parts) > 1:
        parts = [functools.reduce(jnp.add, parts[i:i + 2]) for i in range(0, len(parts), 2)]
    return parts[0]


def folded(wide):
    return functools.reduce(jnp.add, [wide[:, j:j + 128] for j in range(0, wide.shape[1], 128)])


def scaled_product(x, y, scale):
    return lax.dot_general(x, y, NT_DIMS, preferred_element_type=jnp.float32) * scale


def chunk_kernel(scale, parts, earlier, held, *refs):
    x_refs, refs = refs[:parts], refs[parts:]
    y_ref, u_ref, refs = refs[0], refs[1], refs[2:]
    lse_refs, (e_ref, top_ref, lse_ref, wide_ref) = refs[:earlier], refs[earlier:]
    columns = y_ref.shape[0]
    x = jnp.concatenate([r[...] for r in x_refs], axis=0)
    rows = x.shape[0]
    tile = 256
    before = [r[h:h + 1, :] for r in lse_refs for h in range(r.shape[0])]

    def emit(top, total):
        own, sums = [], []
        for h in range(0, rows, 128):
            shift = turned(top[h:h + 128])
            row = jnp.sum(jnp.transpose(total[h:h + 128]), axis=0, keepdims=True)
            top_ref[h // 128:h // 128 + 1, :] = shift
            own.append(shift + jnp.log2(row))
            sums.append(row)
        for h, row in enumerate(before + own):
            if earlier:
                lse_ref[pl.ds(canonical(held, h), 1), :] = row
            else:
                lse_ref[h:h + 1, :] = row
        return functools.reduce(jnp.maximum, sums)

    top, total = None, None
    for j in range(0, columns, tile):
        t = scaled_product(x, y_ref[j:j + tile, :], scale) + u_ref[:, j:j + tile]
        if top is None:
            top = jnp.max(t, axis=1, keepdims=True)
        e = jnp.exp2(t - top)
        e_ref[:, j:j + tile] = e
        total = folded(e) if total is None else total + folded(e)
    largest = emit(top, total)

    @pl.when(jnp.logical_not(jnp.max(largest) < LARGE))
    def _():
        def scores(j):
            place = pl.ds(pl.multiple_of(j * tile, tile), tile)
            return place, scaled_product(x, y_ref[place, :], scale) + u_ref[:, place]

        wide_ref[...] = jnp.full_like(wide_ref, -jnp.inf)

        @pl.loop(0, columns // tile)
        def _(j):
            wide_ref[...] = jnp.maximum(wide_ref[...], jnp.max(scores(j)[1], axis=1, keepdims=True))

        top = wide_ref[:, 0:1]
        wide_ref[...] = jnp.zeros_like(wide_ref)

        @pl.loop(0, columns // tile)
        def _(j):
            place, t = scores(j)
            e = jnp.exp2(t - top)
            e_ref[:, place] = e
            wide_ref[...] += folded(e)

        emit(top, wide_ref[...])


def chunk_call(xs, y, u, held=None, lses=()):
    parts = len(xs)
    width = xs[0].shape[1]
    columns = y.shape[0]
    rows = sum(x.shape[0] for x in xs)
    scale = 2.0 * LOG2E / (width * smoothing)
    listed = rows // 128 + sum(a.shape[0] for a in lses)
    return pl.pallas_call(
        functools.partial(chunk_kernel, scale, parts, len(lses), held),
        in_specs=[WHOLE] * (parts + 2 + len(lses)),
        out_specs=[WHOLE, WHOLE, WHOLE],
        out_shape=[
            jax.ShapeDtypeStruct((rows, columns), jnp.float32),
            jax.ShapeDtypeStruct((rows // 128, 128), jnp.float32),
            jax.ShapeDtypeStruct((listed, 128), jnp.float32),
        ],
        scratch_shapes=[pltpu.VMEM((rows, 128), jnp.float32)],
        compiler_params=params(16),
        cost_estimate=pl.CostEstimate(
            flops=2 * rows * columns * width,
            bytes_accessed=2 * (rows + columns) * width + 4 * rows * columns,
            transcendentals=rows * columns,
        ),
        name="chunk_scores",
    )(*xs, y, u, *lses)


def merge_kernel(first_ref, second_ref, out_ref):
    out_ref[...] = log2_sum([first_ref[...], second_ref[...]])


def merge_call(first, second):
    return pl.pallas_call(
        merge_kernel,
        in_specs=[WHOLE, WHOLE],
        out_specs=WHOLE,
        out_shape=jax.ShapeDtypeStruct(first.shape, jnp.float32),
        compiler_params=params(1),
        cost_estimate=pl.CostEstimate(flops=8 * first.size, bytes_accessed=12 * first.size, transcendentals=0),
        name="merge_rows",
    )(first, second)


def weight_kernel(count, held, *refs):
    top_refs, (stat_ref, logw_ref, base_ref, most_ref) = refs[:count], refs[count:]
    at = 0
    for top_ref in top_refs:
        for r in range(top_ref.shape[0]):
            base_ref[pl.ds(canonical(held, at), 1), :] = top_ref[r:r + 1, :]
            at += 1
    base = base_ref[...] + logw_ref[...] * LOG2E
    bound = base - stat_ref[...]
    most = jnp.max(jnp.max(bound, axis=0, keepdims=True), axis=1, keepdims=True)
    base_ref[...] = base - most
    most_ref[...] = jnp.broadcast_to(most, most_ref.shape)


def weight_call(held, tops, stat, logw):
    shape = jax.ShapeDtypeStruct(stat.shape, jnp.float32)
    return pl.pallas_call(
        functools.partial(weight_kernel, len(tops), held),
        in_specs=[WHOLE] * (len(tops) + 2),
        out_specs=[WHOLE, WHOLE],
        out_shape=[shape, shape],
        compiler_params=params(1),
        cost_estimate=pl.CostEstimate(flops=8 * stat.size, bytes_accessed=16 * stat.size, transcendentals=0),
        name="row_weights",
    )(*tops, stat, logw)


def column_kernel(scale, counts, held, *refs):
    refs = list(refs)
    stat_refs, e_refs, x_refs = [[refs.pop(0) for _ in range(n)] for n in counts]
    base_ref, most_ref, logw_ref, u_ref, y_ref, out_ref, total_ref, v_ref, wide_ref, score_ref = refs
    columns = u_ref.shape[1]
    stats = [r[...] for r in stat_refs]
    top = functools.reduce(jnp.maximum, stats)
    share = functools.reduce(jnp.add, [jnp.exp2(p - top) for p in stats])
    most = most_ref[0:1, :]

    count = base_ref.shape[0]
    part_row = lax.broadcasted_iota(jnp.int32, (4 * count, 128 * count), 0)
    lane_row = lax.broadcasted_iota(jnp.int32, (4 * count, 128 * count), 1) // 128
    pattern = jnp.where(part_row % count == lane_row, 1.0, 0.0).astype(jnp.bfloat16)

    def spread(rows):
        parts = []
        for _ in range(3):
            parts.append(rows.astype(jnp.bfloat16).astype(jnp.float32))
            rows = rows - parts[-1]
        parts = jnp.concatenate(parts + [jnp.zeros_like(rows)], axis=0).astype(jnp.bfloat16)
        laid = lax.dot_general(parts, pattern, (((0,), (0,)), ((), ())), preferred_element_type=jnp.float32)
        for r in range(count):
            wide_ref[r * 128:(r + 1) * 128, :] = laid[:, r * 128:(r + 1) * 128]

    spread(jnp.exp2(base_ref[...] - top) / share)
    total_ref[...] = top + jnp.log2(share)
    starts = [sum(e.shape[0] for e in e_refs[:i]) // 128 for i in range(len(e_refs))]
    places = []
    for e_ref, start in zip(e_refs, starts):
        for r in range(0, e_ref.shape[0], 8):
            if r % 128 == 0:
                from_row = canonical(held, start + r // 128) * 128
            places.append((e_ref, r, pl.ds(pl.multiple_of(from_row + r % 128, 8), 8)))

    strips = columns // 128
    sums = [[] for _ in range(strips)]
    for first in range(0, len(places), 2):
        group = places[first:first + 2]
        weights = [wide_ref[at, :] for _, _, at in group]
        for s, part in enumerate(sums):
            terms = [e_ref[r:r + 8, s * 128:(s + 1) * 128] * a for (e_ref, r, _), a in zip(group, weights)]
            part[:] = [tree_sum(part + [tree_sum(terms)])]
    rows = jnp.concatenate([jnp.sum(part[0], axis=0, keepdims=True) for part in sums], axis=0)
    shifts = jnp.concatenate([u_ref[:, s * 128:(s + 1) * 128] for s in range(strips)], axis=0)
    out_ref[...] = jnp.log2(rows) + (most - shifts)
    least = jnp.min(rows, axis=0, keepdims=True)

    @pl.when(jnp.logical_not(jnp.min(least) > SMALL))
    def _():
        v_ref[...] = logw_ref[...] * LOG2E - total_ref[...]
        spread(v_ref[...])

        @pl.loop(0, columns // 128)
        def _(strip):
            y = y_ref[pl.ds(pl.multiple_of(strip * 128, 128), 128), :]
            at = 0
            for x_ref in x_refs:
                span = slice(at, at + x_ref.shape[0])
                v = wide_ref[pl.ds(pl.multiple_of(canonical(held, at // 128) * 128, 128), 128), :]
                score_ref[span, :] = scaled_product(x_ref[...], y, scale) + v
                at += x_ref.shape[0]
            top = jnp.max(score_ref[...], axis=0, keepdims=True)
            row = jnp.sum(jnp.exp2(score_ref[...] - top), axis=0, keepdims=True)
            out_ref[pl.ds(strip, 1), :] = top + jnp.log2(row)


def column_call(held, stats, exps, pieces, base, most, logw, u, y):
    first = stats[0]
    columns, width = y.shape
    rows = 128 * first.shape[0]
    lists = [stats, exps, pieces]
    scale = 2.0 * LOG2E / (width * smoothing)
    return pl.pallas_call(
        functools.partial(column_kernel, scale, [len(part) for part in lists], held),
        in_specs=[WHOLE] * (sum(len(part) for part in lists) + 5),
        out_specs=[WHOLE, WHOLE],
        out_shape=[
            jax.ShapeDtypeStruct((columns // 128, 128), jnp.float32),
            jax.ShapeDtypeStruct(first.shape, jnp.float32),
        ],
        scratch_shapes=[
            pltpu.VMEM(first.shape, jnp.float32),
            pltpu.VMEM((rows, 128), jnp.float32),
            pltpu.VMEM((rows, 128), jnp.float32),
        ],
        compiler_params=params(20),
        cost_estimate=pl.CostEstimate(
            flops=2 * rows * columns,
            bytes_accessed=4 * rows * columns,
            transcendentals=0,
        ),
        name="column_lse",
    )(*stats, *exps, *pieces, base, most, logw, u, y)


def pot_kernel(inverse, held, parts, total_ref, *refs):
    x_refs, pot_ref = refs[:parts], refs[parts]
    squares = []
    for x_ref in x_refs:
        squares.append(folded(jnp.square(x_ref[...].astype(jnp.float32))))
    squares = jnp.concatenate(squares, axis=0)
    for h in range(squares.shape[0] // 128):
        norm = jnp.sum(jnp.transpose(squares[h * 128:(h + 1) * 128]), axis=0, keepdims=True)
        row = pl.ds(canonical(held, h), 1)
        pot_ref[row, :] = norm * inverse - total_ref[row, :] * LN2


def pot_call(held, total, pieces, inverse):
    return pl.pallas_call(
        functools.partial(pot_kernel, inverse, held, len(pieces)),
        in_specs=[WHOLE] * (1 + len(pieces)),
        out_specs=WHOLE,
        out_shape=jax.ShapeDtypeStruct(total.shape, jnp.float32),
        compiler_params=params(12),
        cost_estimate=pl.CostEstimate(
            flops=2 * sum(x.size for x in pieces),
            bytes_accessed=2 * sum(x.size for x in pieces),
            transcendentals=0,
        ),
        name="treated_pot",
    )(total, *pieces)


def body(chips, treated_emb, control_emb, control_pot, control_logw, treated_logw):
    width = control_emb.shape[1]
    inverse = 1.0 / (width * smoothing)
    control_sq = jnp.sum(jnp.square(control_emb.astype(jnp.float32)), axis=1) * inverse
    u = ((control_pot + control_logw - control_sq) * LOG2E)[None, :]
    logw = treated_logw.reshape(-1, 128)
    rows = treated_emb.shape[0]
    ring = chips == 4 and rows == 128

    def moved(value, target):
        perm = [(z * 2 + c, target(z, c)) for z in range(chips) for c in range(2)]
        return lax.ppermute(value, "control", perm)

    def swapped(value):
        return moved(value, lambda z, c: z * 2 + 1 - c)

    def shifted(value, shift):
        return moved(value, lambda z, c: (z + shift) % chips * 2 + c)

    if ring:
        held = (chips, ((0, 0), (0, 1), (1, 0), (3, 0), (1, 1), (3, 1), (2, 0), (2, 1)))
        x0 = treated_emb
        x1 = shifted(x0, 1)
        p0 = swapped(x0)
        behind, u = lax.optimization_barrier((x0, u))
        x3 = shifted(behind, 3)
        e0, top0, lse0 = chunk_call([x0, p0], control_emb, u)
        x1, lse0 = lax.optimization_barrier((x1, lse0))
        x2 = shifted(x1, 1)
        x1, x3 = lax.optimization_barrier((x1, x3))
        e1, top1, lse1 = chunk_call([x1, x3], control_emb, u)
        x1, x3, lse1 = lax.optimization_barrier((x1, x3, lse1))
        p1 = swapped(x1)
        p3 = swapped(x3)
        p1, p3, x2 = lax.optimization_barrier((p1, p3, x2))
        p2 = swapped(x2)
        e2, top2, lse2 = chunk_call([p1, p3], control_emb, u)
        p2, lse2 = lax.optimization_barrier((p2, lse2))
        e3, top3, stats = chunk_call([x2, p2], control_emb, u, held, [lse0, lse1, lse2])
        exps, tops = [e0, e1, e2, e3], [top0, top1, top2, top3]
        pieces = [x0, p0, x1, x3, p1, p3, x2, p2]
        chip_stats = merge_call(stats, swapped(stats))
        stats = [chip_stats]
        for flip in (1, 2, 3):
            stats.append(moved(chip_stats, lambda z, c: (z ^ flip) * 2 + c))
    else:
        held = None
        block = lax.all_gather(treated_emb, "control", axis=0, tiled=True)
        pieces = [block[i:i + 128] for i in range(0, block.shape[0], 128)]
        exps, tops, lses = [], [], []
        for k in range(0, len(pieces), 2):
            e, top, lse = chunk_call(pieces[k:k + 2], control_emb, u)
            exps.append(e)
            tops.append(top)
            lses.append(lse)
        gathered = lax.all_gather(jnp.concatenate(lses, axis=0), "control")
        top = jnp.max(gathered, axis=0)
        stats = [top + jnp.log2(jnp.sum(jnp.exp2(gathered - top[None]), axis=0))]

    if ring:
        pieces = list(lax.optimization_barrier((tuple(pieces), stats[-1]))[0])
    base, most = weight_call(held, tops, stats[0], logw)
    column, total = column_call(held, stats, exps, pieces, base, most, logw, u, control_emb)
    treated_pot = pot_call(held, total, pieces, inverse).reshape(-1)

    size = lax.axis_size("treated")
    if size == 4:
        parts = [column]
        for flip in (1, 2, 3):
            parts.append(lax.ppermute(column, "treated", [(s, s ^ flip) for s in range(size)]))
    else:
        gathered = lax.all_gather(column, "treated")
        parts = [gathered[s] for s in range(size)]
    column_lse = log2_sum(parts).reshape(-1) * LN2 - control_sq
    return (treated_pot, column_lse)


def solution(mesh):
    placed = (
        P(("treated", "control"), None),
        P("control", None),
        P("control"),
        P("control"),
        P("treated"),
    )
    return jax.shard_map(
        functools.partial(body, mesh.shape["control"] // 2),
        mesh=mesh,
        in_specs=placed,
        out_specs=(P("treated"), P("control")),
        check_vma=False,
    )
```

time: 121 us -> 77.1 us (0.64)
  blocking collectives: 45.3 us -> 0 us
  Pallas kernels: 0 us -> 41.8 us
  waiting for transfers between devices: 30.4 us -> 7.76 us
  starting transfers between devices: 0.04 us -> 21 us
  other arithmetic: 19.8 us -> 4.41 us
  between operations: 14.1 us -> 0.76 us
  matrix products: 11 us -> 0 us
    pallas_call x0 -> x8, Pallas kernels: none -> 41.8 us  [the longest x4 25.2 us: chunk_call(): pl.pallas_call(functools.partial(chunk_kernel, scale, parts, len(lses), h...]
    all_gather x1 -> x0, waiting for transfers between devices: 29.7 us -> none  [body(): slab_block = lax.all_gather(treated_emb, 'control', axis=0, tiled=True)]
    ppermute x0 -> x14, starting transfers between devices: none -> 21 us  [the longest x11 17.5 us: moved(): return lax.ppermute(value, 'control', perm)]
    all_gather x2 -> x0, blocking collectives: 16.2 us -> none  [combined_all(): gathered = jax.tree.map(lambda a: lax.all_gather(a, axis), part)]
    pmax x1 -> x0, blocking collectives: 15.5 us -> none  [body(): highest = lax.pmax(jnp.max(row_scores, axis=1), 'control')]
    psum x1 -> x0, blocking collectives: 13.6 us -> none  [body(): lax.psum(jnp.sum(jnp.exp(row_scores - highest[:, None]), axis=1), 'control')]
    dot_general x1 -> x0, matrix products: 11 us -> none  [body(): lax.dot_general(slab_block, control_emb, (((1,), (1,)), ((), ())), prefer...]
    reduce_sum x4 -> x1, other arithmetic: 13.8 us -> 3.07 us  [body(): jnp.sum(jnp.square(control_emb.astype(jnp.float32)), axis=1) * inverse]
  transfers between devices with their start and end apart: 1 -> 14, of which waited for: 1 -> 7; matrix products, arithmetic and copies ran while one was open for 3% -> 5% of each run, Pallas kernels for 0% -> 24%
where the time goes in v1:
time: 77.1 us; the launch traced here: 76.7 us
  Pallas kernels  41.8 us (54%)
  starting transfers between devices  21 us (27%)
  waiting for transfers between devices  7.76 us (10%)
  other arithmetic  4.41 us (6%)
  local copies, waits for them, and re-layouts  1 us (1%)
    pallas_call x4, Pallas kernels, chunk_call(): pl.pallas_call(functools.partial(chunk_kernel, scale, parts, len(lses), h...  25.2 us
    ppermute x11, starting transfers between devices, moved(): return lax.ppermute(value, 'control', perm)  17.5 us
    pallas_call x1, Pallas kernels, column_call(): pl.pallas_call(functools.partial(column_kernel, scale, [len(part) for par...  15.4 us
    ppermute x11, waiting for transfers between devices, moved(): return lax.ppermute(value, 'control', perm)  6 us
    ppermute x3, starting transfers between devices, body(): lax.ppermute(column, 'treated', [(s, s ^ flip) for s in range(size)])  3.55 us
    reduce_sum x1, other arithmetic, body(): jnp.sum(jnp.square(control_emb.astype(jnp.float32)), axis=1) * inverse  3.07 us
    ppermute x3, waiting for transfers between devices, body(): lax.ppermute(column, 'treated', [(s, s ^ flip) for s in range(size)])  1.77 us
  transfers between devices with their start and end apart: 14, of which 7 were waited for; matrix products, arithmetic and copies ran while one was open for 5% of the time, Pallas kernels for 24%

profile of v1, /device:TPU:0, one launch (start us, length us, event | category | flops | bytes accessed | tf_op | source)
XLA Modules:
  0.0 76.7 jit_solution(11788687415399304689)
XLA Ops:
  0.6 0.0 copy-start
  0.6 0.0 copy-start.4
  0.6 0.5 collective-permute-start.1
  1.2 2.6 %collective-permute-start = (bf16[128,1024]{1,0:T(8,128)(2,1)}, bf16[128,1024]{1,0:T(8,128)(2,1)S(1)}, u32[]{:S(2)}, u32[]{:S(2)}) collective-permute-start(bf16[128,1024]{1,0:T(8,128)(2,1)} %refs_0_.2), channel_id=1, source_target_pairs={{0,2},{1,3},{2,4},{3,5},{4,6},{5,7},{6,0},{7,1},{8,10},{9,11},{10,... | collective-permute-start | bytes 786440 | tf_op jit(solution)/shard_map/ppermute | solution.py:321
  3.8 3.1 %multiply_reduce_fusion = f32[2048]{0:T(1024)S(1)} fusion(bf16[2048,1024]{1,0:T(8,128)(2,1)} %refs_20_.1), kind=kLoop, calls=%fused_computation | loop fusion | flops 6289408 | bytes 4202496 | tf_op jit(solution)/shard_map/reduce_sum | solution.py:313
  6.9 0.0 copy-done.4
  6.9 0.7 subtract_multiply_fusion
  7.6 2.2 %collective-permute-start.2 = (bf16[128,1024]{1,0:T(8,128)(2,1)}, bf16[128,1024]{1,0:T(8,128)(2,1)S(1)}, u32[]{:S(2)}, u32[]{:S(2)}) collective-permute-start(bf16[128,1024]{1,0:T(8,128)(2,1)} %refs_0_.2), channel_id=1, source_target_pairs={{0,6},{1,7},{2,0},{3,1},{4,2},{5,3},{6,4},{7,5},{8,14},{9,15},{10,... | collective-permute-start | bytes 786440 | tf_op jit(solution)/shard_map/ppermute | solution.py:321
  9.8 0.0 collective-permute-done.1.refs_1_.refs_9_
  9.8 0.0 copy-done
  9.8 0.0 copy-start.1
  9.8 1.0 %copy-done.1 = bf16[128,1024]{1,0:T(8,128)(2,1)S(1)} copy-done((bf16[128,1024]{1,0:T(8,128)(2,1)S(1)}, bf16[128,1024]{1,0:T(8,128)(2,1)}, u32[]{:S(2)}) %copy-start.1) | copy-done | bytes 262168
  10.8 7.9 %chunk_scores.4 = (f32[256,2048]{1,0:T(8,128)S(1)}, f32[2,128]{1,0:T(2,128)S(1)}, f32[2,128]{1,0:T(2,128)S(1)}) custom-call(bf16[128,1024]{1,0:T(8,128)(2,1)S(1)} %copy-done.1, bf16[128,1024]{1,0:T(8,128)(2,1)S(1)} %collective-permute-done.1.refs_1_.refs_9_, bf16[2048,1024]{1,0:T(8,128)(2,1)S(1)} %copy-done, f32[1,2048]{1,0:T(1,128)S(1)} %bitcast.5), custom_call_target="tpu_custom_call" | custom-call | flops 1073741824 | bytes 6815744 | tf_op jit(solution)/shard_map/chunk_scores/pallas_call | solution.py:123
  18.7 0.0 collective-permute-done.refs_0_.refs_10_.refs_2_
  18.7 0.1 collective-permute-start.5
  18.8 0.0 collective-permute-done.2.refs_1_.refs_11_.refs_3_
  18.8 7.9 %chunk_scores.5 = (f32[256,2048]{1,0:T(8,128)S(1)}, f32[2,128]{1,0:T(2,128)S(1)}, f32[2,128]{1,0:T(2,128)S(1)}) custom-call(bf16[128,1024]{1,0:T(8,128)(2,1)S(1)} %collective-permute-done.refs_0_.refs_10_.refs_2_, bf16[128,1024]{1,0:T(8,128)(2,1)S(1)} %collective-permute-done.2.refs_1_.refs_11_.refs_3_, bf16[2048,1024]{1,0:T(8,128)(2,1)S(1)} %copy-done, ...), custom_call_target="tpu_custom_call" | custom-call | flops 1073741824 | bytes 6815744 | tf_op jit(solution)/shard_map/chunk_scores/pallas_call | solution.py:123
  26.7 0.0 copy-start.3
  26.7 0.0 copy-start.2
  26.7 0.1 collective-permute-start.3
  26.8 0.5 collective-permute-start.4
  27.3 0.0 collective-permute-done.5.refs_0_.refs_14_.refs_6_
  27.3 1.0 %collective-permute-done.3.refs_0_.refs_12_.refs_4_ = bf16[128,1024]{1,0:T(8,128)(2,1)S(1)} collective-permute-done((bf16[128,1024]{1,0:T(8,128)(2,1)S(1)}, bf16[128,1024]{1,0:T(8,128)(2,1)S(1)}, u32[]{:S(2)}, u32[]{:S(2)}) %collective-permute-start.3) | collective-permute-done | bytes 262176 | tf_op jit(solution)/shard_map/ppermute | solution.py:321
  28.3 0.4 collective-permute-done.4.refs_1_.refs_13_.refs_5_
  28.7 0.1 collective-permute-start.6
  28.8 1.5 %chunk_scores.6 = (f32[256,2048]{1,0:T(8,128)S(1)}, f32[2,128]{1,0:T(2,128)S(1)}, f32[2,128]{1,0:T(2,128)S(1)}) custom-call(bf16[128,1024]{1,0:T(8,128)(2,1)S(1)} %collective-permute-done.3.refs_0_.refs_12_.refs_4_, bf16[128,1024]{1,0:T(8,128)(2,1)S(1)} %collective-permute-done.4.refs_1_.refs_13_.refs_5_, bf16[2048,1024]{1,0:T(8,128)(2,1)S(1)} %copy-done, ...), custom_call_target="tpu_custom_call" | custom-call | flops 1073741824 | bytes 6815744 | tf_op jit(solution)/shard_map/chunk_scores/pallas_call | solution.py:123
  30.3 0.0 collective-permute-done.6.refs_1_.refs_15_.refs_7_
  30.3 7.9 %chunk_scores.7 = (f32[256,2048]{1,0:T(8,128)S(1)}, f32[2,128]{1,0:T(2,128)S(1)}, f32[8,128]{1,0:T(8,128)S(1)}) custom-call(bf16[128,1024]{1,0:T(8,128)(2,1)S(1)} %collective-permute-done.5.refs_0_.refs_14_.refs_6_, bf16[128,1024]{1,0:T(8,128)(2,1)S(1)} %collective-permute-done.6.refs_1_.refs_15_.refs_7_, bf16[2048,1024]{1,0:T(8,128)(2,1)S(1)} %copy-done, ...), custom_call_target="tpu_custom_call" | custom-call | flops 1073741824 | bytes 6815744 | tf_op jit(solution)/shard_map/chunk_scores/pallas_call | solution.py:123
  38.3 6.9 %collective-permute-start.7 = (f32[8,128]{1,0:T(8,128)S(1)}, f32[8,128]{1,0:T(8,128)S(1)}, u32[]{:S(2)}, u32[]{:S(2)}) collective-permute-start(f32[8,128]{1,0:T(8,128)S(1)} %get-tuple-element.57.first_ref), channel_id=1, source_target_pairs={{0,1},{1,0},{2,3},{3,2},{4,5},{5,4},{6,7},{7,6},{8,9},{9,8},{10,11... | collective-permute-start | bytes 12296 | tf_op jit(solution)/shard_map/ppermute | solution.py:321
  45.1 0.8 %collective-permute-done.7.second_ref = f32[8,128]{1,0:T(8,128)S(1)} collective-permute-done((f32[8,128]{1,0:T(8,128)S(1)}, f32[8,128]{1,0:T(8,128)S(1)}, u32[]{:S(2)}, u32[]{:S(2)}) %collective-permute-start.7) | collective-permute-done | bytes 4128 | tf_op jit(solution)/shard_map/ppermute | solution.py:321
  46.0 3.8 %collective-permute-start.10 = (f32[8,128]{1,0:T(8,128)S(1)}, f32[8,128]{1,0:T(8,128)S(1)}, u32[]{:S(2)}, u32[]{:S(2)}) collective-permute-start(f32[8,128]{1,0:T(8,128)S(1)} %merge_rows.1.refs_4_.refs_0_), channel_id=1, source_target_pairs={{0,6},{1,7},{2,4},{3,5},{4,2},{5,3},{6,0},{7,1},{8,14},{9,15},{10,... | collective-permute-start | bytes 12296 | tf_op jit(solution)/shard_map/ppermute | solution.py:321
  49.8 0.0 collective-permute-start.9
  49.8 0.6 collective-permute-start.8
  50.4 0.0 copy-done.3
  50.4 0.1 row_weights.1
  50.5 0.9 %collective-permute-done.10.refs_3_ = f32[8,128]{1,0:T(8,128)S(1)} collective-permute-done((f32[8,128]{1,0:T(8,128)S(1)}, f32[8,128]{1,0:T(8,128)S(1)}, u32[]{:S(2)}, u32[]{:S(2)}) %collective-permute-start.10) | collective-permute-done | bytes 4128 | tf_op jit(solution)/shard_map/ppermute | solution.py:321
  51.4 2.9 %collective-permute-done.9.refs_2_ = f32[8,128]{1,0:T(8,128)S(1)} collective-permute-done((f32[8,128]{1,0:T(8,128)S(1)}, f32[8,128]{1,0:T(8,128)S(1)}, u32[]{:S(2)}, u32[]{:S(2)}) %collective-permute-start.9) | collective-permute-done | bytes 4128 | tf_op jit(solution)/shard_map/ppermute | solution.py:321
  54.3 0.0 collective-permute-done.8.refs_1_
  54.3 0.0 copy-done.2
  54.3 15.4 %column_lse.1 = (f32[16,128]{1,0:T(8,128)S(1)}, f32[8,128]{1,0:T(8,128)S(1)}) custom-call(f32[8,128]{1,0:T(8,128)S(1)} %merge_rows.1.refs_4_.refs_0_, f32[8,128]{1,0:T(8,128)S(1)} %collective-permute-done.8.refs_1_, f32[8,128]{1,0:T(8,128)S(1)} %collective-permute-done.9.refs_2_, f32[8,128]{1,0:T(8,128)S(1)} %collective-permute-done.10.refs_3_, ...), custom_call_target="tpu_custom_call" | custom-call | flops 4194304 | bytes 8388608 | tf_op jit(solution)/shard_map/column_lse/pallas_call | solution.py:259
  69.7 2.6 %collective-permute-start.13 = (f32[16,128]{1,0:T(8,128)S(1)}, f32[16,128]{1,0:T(8,128)S(1)}, u32[]{:S(2)}, u32[]{:S(2)}) collective-permute-start(f32[16,128]{1,0:T(8,128)S(1)} %get-tuple-element.77), channel_id=1, source_target_pairs={{0,24},{8,16},{16,8},{24,0},{1,25},{9,17},{17,9},{25,1},{2,26},{10... | collective-permute-start | bytes 24584 | tf_op jit(solution)/shard_map/ppermute | solution.py:379
  72.2 0.2 collective-permute-start.12
  72.4 0.8 %collective-permute-start.11 = (f32[16,128]{1,0:T(8,128)S(1)}, f32[16,128]{1,0:T(8,128)S(1)}, u32[]{:S(2)}, u32[]{:S(2)}) collective-permute-start(f32[16,128]{1,0:T(8,128)S(1)} %get-tuple-element.77), channel_id=1, source_target_pairs={{0,8},{8,0},{16,24},{24,16},{1,9},{9,1},{17,25},{25,17},{2,10},{10... | collective-permute-start | bytes 24584 | tf_op jit(solution)/shard_map/ppermute | solution.py:379
  73.2 1.1 %treated_pot.1 = f32[8,128]{1,0:T(8,128)} custom-call(f32[8,128]{1,0:T(8,128)S(1)} %get-tuple-element.76.total_ref, bf16[128,1024]{1,0:T(8,128)(2,1)S(1)} %copy-done.2, bf16[128,1024]{1,0:T(8,128)(2,1)S(1)} %collective-permute-done.1.refs_1_.refs_9_, bf16[128,1024]{1,0:T(8,128)(2,1)S(1)} %collective-permute-done.refs_0_.refs_10_.refs_2_, ...), custom_call_target="tpu_custom_call" | custom-call | flops 2097152 | bytes 2097152 | tf_op jit(solution)/shard_map/treated_pot/pallas_call | solution.py:295
  74.3 0.0 collective-permute-done.13
  74.3 1.6 %collective-permute-done.12 = f32[16,128]{1,0:T(8,128)S(1)} collective-permute-done((f32[16,128]{1,0:T(8,128)S(1)}, f32[16,128]{1,0:T(8,128)S(1)}, u32[]{:S(2)}, u32[]{:S(2)}) %collective-permute-start.12) | collective-permute-done | bytes 8224 | tf_op jit(solution)/shard_map/ppermute | solution.py:379
  75.9 0.2 collective-permute-done.11
  76.1 0.6 bitcast_subtract_fusion
  (1 shorter events, 0.0 us)
Async XLA Ops:
  0.6 9.2 %copy-start = (bf16[2048,1024]{1,0:T(8,128)(2,1)S(1)}, bf16[2048,1024]{1,0:T(8,128)(2,1)}, u32[]{:S(2)}) copy-start(bf16[2048,1024]{1,0:T(8,128)(2,1)} %refs_20_.1) | copy-start | bytes 12582916
  0.6 6.2 %copy-start.4 = (f32[2048]{0:T(1024)S(1)}, f32[2048]{0:T(1024)}, u32[]{:S(2)}) copy-start(f32[2048]{0:T(1024)} %param.7) | copy-start | bytes 24580
  0.6 9.1 %collective-permute-start.1 = (bf16[128,1024]{1,0:T(8,128)(2,1)}, bf16[128,1024]{1,0:T(8,128)(2,1)S(1)}, u32[]{:S(2)}, u32[]{:S(2)}) collective-permute-start(bf16[128,1024]{1,0:T(8,128)(2,1)} %refs_0_.2), channel_id=1, source_target_pairs={{0,1},{1,0},{2,3},{3,2},{4,5},{5,4},{6,7},{7,6},{8,9},{9,8},{10,11... | collective-permute-start | bytes 786440 | tf_op jit(solution)/shard_map/ppermute | solution.py:321
  1.2 17.5 %collective-permute-start = (bf16[128,1024]{1,0:T(8,128)(2,1)}, bf16[128,1024]{1,0:T(8,128)(2,1)S(1)}, u32[]{:S(2)}, u32[]{:S(2)}) collective-permute-start(bf16[128,1024]{1,0:T(8,128)(2,1)} %refs_0_.2), channel_id=1, source_target_pairs={{0,2},{1,3},{2,4},{3,5},{4,6},{5,7},{6,0},{7,1},{8,10},{9,11},{10,... | collective-permute-start | bytes 786440 | tf_op jit(solution)/shard_map/ppermute | solution.py:321
  7.6 11.2 %collective-permute-start.2 = (bf16[128,1024]{1,0:T(8,128)(2,1)}, bf16[128,1024]{1,0:T(8,128)(2,1)S(1)}, u32[]{:S(2)}, u32[]{:S(2)}) collective-permute-start(bf16[128,1024]{1,0:T(8,128)(2,1)} %refs_0_.2), channel_id=1, source_target_pairs={{0,6},{1,7},{2,0},{3,1},{4,2},{5,3},{6,4},{7,5},{8,14},{9,15},{10,... | collective-permute-start | bytes 786440 | tf_op jit(solution)/shard_map/ppermute | solution.py:321
  9.8 1.0 %copy-start.1 = (bf16[128,1024]{1,0:T(8,128)(2,1)S(1)}, bf16[128,1024]{1,0:T(8,128)(2,1)}, u32[]{:S(2)}) copy-start(bf16[128,1024]{1,0:T(8,128)(2,1)} %refs_0_.2) | copy-start | bytes 786436
  18.7 8.6 %collective-permute-start.5 = (bf16[128,1024]{1,0:T(8,128)(2,1)S(1)}, bf16[128,1024]{1,0:T(8,128)(2,1)S(1)}, u32[]{:S(2)}, u32[]{:S(2)}) collective-permute-start(bf16[128,1024]{1,0:T(8,128)(2,1)S(1)} %collective-permute-done.refs_0_.refs_10_.refs_2_), channel_id=1, source_target_pairs={{0,2},{1,3},{2,4},{3,5},{4,6},{5,7},{6,0},{7,1},{8,10},{9,11},{10,... | collective-permute-start | bytes 786440 | tf_op jit(solution)/shard_map/ppermute | solution.py:321
  26.7 23.8 %copy-start.3 = (f32[1024]{0:T(1024)S(1)}, f32[1024]{0:T(1024)}, u32[]{:S(2)}) copy-start(f32[1024]{0:T(1024)} %param.9) | copy-start | bytes 12292
  26.7 27.6 %copy-start.2 = (bf16[128,1024]{1,0:T(8,128)(2,1)S(1)}, bf16[128,1024]{1,0:T(8,128)(2,1)}, u32[]{:S(2)}) copy-start(bf16[128,1024]{1,0:T(8,128)(2,1)} %refs_0_.2) | copy-start | bytes 786436
  26.7 1.6 %collective-permute-start.3 = (bf16[128,1024]{1,0:T(8,128)(2,1)S(1)}, bf16[128,1024]{1,0:T(8,128)(2,1)S(1)}, u32[]{:S(2)}, u32[]{:S(2)}) collective-permute-start(bf16[128,1024]{1,0:T(8,128)(2,1)S(1)} %collective-permute-done.refs_0_.refs_10_.refs_2_), channel_id=1, source_target_pairs={{0,1},{1,0},{2,3},{3,2},{4,5},{5,4},{6,7},{7,6},{8,9},{9,8},{10,11... | collective-permute-start | bytes 786440 | tf_op jit(solution)/shard_map/ppermute | solution.py:321
  26.8 1.9 %collective-permute-start.4 = (bf16[128,1024]{1,0:T(8,128)(2,1)S(1)}, bf16[128,1024]{1,0:T(8,128)(2,1)S(1)}, u32[]{:S(2)}, u32[]{:S(2)}) collective-permute-start(bf16[128,1024]{1,0:T(8,128)(2,1)S(1)} %collective-permute-done.2.refs_1_.refs_11_.refs_3_), channel_id=1, source_target_pairs={{0,1},{1,0},{2,3},{3,2},{4,5},{5,4},{6,7},{7,6},{8,9},{9,8},{10,11... | collective-permute-start | bytes 786440 | tf_op jit(solution)/shard_map/ppermute | solution.py:321
  28.7 1.7 %collective-permute-start.6 = (bf16[128,1024]{1,0:T(8,128)(2,1)S(1)}, bf16[128,1024]{1,0:T(8,128)(2,1)S(1)}, u32[]{:S(2)}, u32[]{:S(2)}) collective-permute-start(bf16[128,1024]{1,0:T(8,128)(2,1)S(1)} %collective-permute-done.5.refs_0_.refs_14_.refs_6_), channel_id=1, source_target_pairs={{0,1},{1,0},{2,3},{3,2},{4,5},{5,4},{6,7},{7,6},{8,9},{9,8},{10,11... | collective-permute-start | bytes 786440 | tf_op jit(solution)/shard_map/ppermute | solution.py:321
  38.3 7.7 %collective-permute-start.7 = (f32[8,128]{1,0:T(8,128)S(1)}, f32[8,128]{1,0:T(8,128)S(1)}, u32[]{:S(2)}, u32[]{:S(2)}) collective-permute-start(f32[8,128]{1,0:T(8,128)S(1)} %get-tuple-element.57.first_ref), channel_id=1, source_target_pairs={{0,1},{1,0},{2,3},{3,2},{4,5},{5,4},{6,7},{7,6},{8,9},{9,8},{10,11... | collective-permute-start | bytes 12296 | tf_op jit(solution)/shard_map/ppermute | solution.py:321
  46.0 5.5 %collective-permute-start.10 = (f32[8,128]{1,0:T(8,128)S(1)}, f32[8,128]{1,0:T(8,128)S(1)}, u32[]{:S(2)}, u32[]{:S(2)}) collective-permute-start(f32[8,128]{1,0:T(8,128)S(1)} %merge_rows.1.refs_4_.refs_0_), channel_id=1, source_target_pairs={{0,6},{1,7},{2,4},{3,5},{4,2},{5,3},{6,0},{7,1},{8,14},{9,15},{10,... | collective-permute-start | bytes 12296 | tf_op jit(solution)/shard_map/ppermute | solution.py:321
  49.8 4.5 %collective-permute-start.9 = (f32[8,128]{1,0:T(8,128)S(1)}, f32[8,128]{1,0:T(8,128)S(1)}, u32[]{:S(2)}, u32[]{:S(2)}) collective-permute-start(f32[8,128]{1,0:T(8,128)S(1)} %merge_rows.1.refs_4_.refs_0_), channel_id=1, source_target_pairs={{0,4},{1,5},{2,6},{3,7},{4,0},{5,1},{6,2},{7,3},{8,12},{9,13},{10,... | collective-permute-start | bytes 12296 | tf_op jit(solution)/shard_map/ppermute | solution.py:321
  49.8 4.5 %collective-permute-start.8 = (f32[8,128]{1,0:T(8,128)S(1)}, f32[8,128]{1,0:T(8,128)S(1)}, u32[]{:S(2)}, u32[]{:S(2)}) collective-permute-start(f32[8,128]{1,0:T(8,128)S(1)} %merge_rows.1.refs_4_.refs_0_), channel_id=1, source_target_pairs={{0,2},{1,3},{2,0},{3,1},{4,6},{5,7},{6,4},{7,5},{8,10},{9,11},{10,... | collective-permute-start | bytes 12296 | tf_op jit(solution)/shard_map/ppermute | solution.py:321
  69.7 4.6 %collective-permute-start.13 = (f32[16,128]{1,0:T(8,128)S(1)}, f32[16,128]{1,0:T(8,128)S(1)}, u32[]{:S(2)}, u32[]{:S(2)}) collective-permute-start(f32[16,128]{1,0:T(8,128)S(1)} %get-tuple-element.77), channel_id=1, source_target_pairs={{0,24},{8,16},{16,8},{24,0},{1,25},{9,17},{17,9},{25,1},{2,26},{10... | collective-permute-start | bytes 24584 | tf_op jit(solution)/shard_map/ppermute | solution.py:379
  72.2 3.7 %collective-permute-start.12 = (f32[16,128]{1,0:T(8,128)S(1)}, f32[16,128]{1,0:T(8,128)S(1)}, u32[]{:S(2)}, u32[]{:S(2)}) collective-permute-start(f32[16,128]{1,0:T(8,128)S(1)} %get-tuple-element.77), channel_id=1, source_target_pairs={{0,16},{8,24},{16,0},{24,8},{1,17},{9,25},{17,1},{25,9},{2,18},{10... | collective-permute-start | bytes 24584 | tf_op jit(solution)/shard_map/ppermute | solution.py:379
  72.4 3.7 %collective-permute-start.11 = (f32[16,128]{1,0:T(8,128)S(1)}, f32[16,128]{1,0:T(8,128)S(1)}, u32[]{:S(2)}, u32[]{:S(2)}) collective-permute-start(f32[16,128]{1,0:T(8,128)S(1)} %get-tuple-element.77), channel_id=1, source_target_pairs={{0,8},{8,0},{16,24},{24,16},{1,9},{9,1},{17,25},{25,17},{2,10},{10... | collective-permute-start | bytes 24584 | tf_op jit(solution)/shard_map/ppermute | solution.py:379

commit v2 on v1

--- a/solution.py
+++ b/solution.py
@@ -113,7 +113,7 @@
         emit(top, wide_ref[...])
 
 
-def chunk_call(xs, y, u, held=None, lses=()):
+def chunk_call(xs, y, u, held=None, lses=(), hidden=False):
     parts = len(xs)
     width = xs[0].shape[1]
     columns = y.shape[0]
@@ -132,12 +132,32 @@
         scratch_shapes=[pltpu.VMEM((rows, 128), jnp.float32)],
         compiler_params=params(16),
         cost_estimate=pl.CostEstimate(
-            flops=2 * rows * columns * width,
-            bytes_accessed=2 * (rows + columns) * width + 4 * rows * columns,
-            transcendentals=rows * columns,
+            flops=0 if hidden else 2 * rows * columns * width,
+            bytes_accessed=0 if hidden else 2 * (rows + columns) * width + 4 * rows * columns,
+            transcendentals=0 if hidden else rows * columns,
         ),
         name="chunk_scores",
     )(*xs, y, u, *lses)
+
+
+def halves_kernel(count, *refs):
+    for x_ref, first_ref, second_ref in zip(refs[:count], refs[count::2], refs[count + 1::2]):
+        half = first_ref.shape[0]
+        first_ref[...] = x_ref[:half, :]
+        second_ref[...] = x_ref[half:, :]
+
+
+def halves_call(xs):
+    half = jax.ShapeDtypeStruct((xs[0].shape[0] // 2, xs[0].shape[1]), xs[0].dtype)
+    return pl.pallas_call(
+        functools.partial(halves_kernel, len(xs)),
+        in_specs=[WHOLE] * len(xs),
+        out_specs=[WHOLE] * (2 * len(xs)),
+        out_shape=[half] * (2 * len(xs)),
+        compiler_params=params(4),
+        cost_estimate=pl.CostEstimate(flops=0, bytes_accessed=0, transcendentals=0),
+        name="halves",
+    )(*xs)
 
 
 def merge_kernel(first_ref, second_ref, out_ref):
@@ -242,7 +262,8 @@
             at = 0
             for x_ref in x_refs:
                 span = slice(at, at + x_ref.shape[0])
-                v = wide_ref[pl.ds(pl.multiple_of(canonical(held, at // 128) * 128, 128), 128), :]
+                from_row = canonical(held, at // 128) * 128 + at % 128
+                v = wide_ref[pl.ds(pl.multiple_of(from_row, 8), x_ref.shape[0]), :]
                 score_ref[span, :] = scaled_product(x_ref[...], y, scale) + v
                 at += x_ref.shape[0]
             top = jnp.max(score_ref[...], axis=0, keepdims=True)
@@ -327,7 +348,7 @@
         return moved(value, lambda z, c: (z + shift) % chips * 2 + c)
 
     if ring:
-        held = (chips, ((0, 0), (0, 1), (1, 0), (3, 0), (1, 1), (3, 1), (2, 0), (2, 1)))
+        held = (chips, ((0, 0), (0, 1), (1, 0), (1, 1), (3, 0), (3, 1), (2, 0), (2, 1)))
         x0 = treated_emb
         x1 = shifted(x0, 1)
         p0 = swapped(x0)
@@ -336,18 +357,16 @@
         e0, top0, lse0 = chunk_call([x0, p0], control_emb, u)
         x1, lse0 = lax.optimization_barrier((x1, lse0))
         x2 = shifted(x1, 1)
-        x1, x3 = lax.optimization_barrier((x1, x3))
-        e1, top1, lse1 = chunk_call([x1, x3], control_emb, u)
-        x1, x3, lse1 = lax.optimization_barrier((x1, x3, lse1))
-        p1 = swapped(x1)
-        p3 = swapped(x3)
-        p1, p3, x2 = lax.optimization_barrier((p1, p3, x2))
+        p1 = [swapped(part) for part in halves_call([x1])]
+        e1, top1, lse1 = chunk_call([x1, *p1], control_emb, u, hidden=True)
+        x3, lse1 = lax.optimization_barrier((x3, lse1))
+        p3 = [swapped(part) for part in halves_call([x3])]
+        e2, top2, lse2 = chunk_call([x3, *p3], control_emb, u, hidden=True)
+        x2, lse2 = lax.optimization_barrier((x2, lse2))
         p2 = swapped(x2)
-        e2, top2, lse2 = chunk_call([p1, p3], control_emb, u)
-        p2, lse2 = lax.optimization_barrier((p2, lse2))
         e3, top3, stats = chunk_call([x2, p2], control_emb, u, held, [lse0, lse1, lse2])
         exps, tops = [e0, e1, e2, e3], [top0, top1, top2, top3]
-        pieces = [x0, p0, x1, x3, p1, p3, x2, p2]
+        pieces = [x0, p0, x1, *p1, x3, *p3, x2, p2]
         chip_stats = merge_call(stats, swapped(stats))
         stats = [chip_stats]
         for flip in (1, 2, 3):

time: 77.1 us -> 82.9 us (1.075)
  Pallas kernels: 41.8 us -> 52.2 us
  starting transfers between devices: 21 us -> 15.2 us
  waiting for transfers between devices: 7.76 us -> 9.03 us
    pallas_call x4, Pallas kernels: 25.2 us -> 31.6 us  [chunk_call(): pl.pallas_call(functools.partial(chunk_kernel, scale, parts, len(lses), h...]
    ppermute x11 -> x13, starting transfers between devices: 17.5 us -> 11.7 us  [moved(): return lax.ppermute(value, 'control', perm)]
    pallas_call x1, Pallas kernels: 15.4 us -> 19.3 us  [column_call(): pl.pallas_call(functools.partial(column_kernel, scale, [len(part) for par...]
    ppermute x11 -> x13, waiting for transfers between devices: 6 us -> 6.96 us  [moved(): return lax.ppermute(value, 'control', perm)]
  transfers between devices with their start and end apart: 14 -> 16, of which waited for: 7 -> 10; matrix products, arithmetic and copies ran while one was open for 5% -> 5% of each run, Pallas kernels for 24% -> 30%
where the time goes in v2:
time: 82.9 us; the launch traced here: 82.6 us
  Pallas kernels  52.2 us (63%)
  starting transfers between devices  15.2 us (18%)
  waiting for transfers between devices  9.03 us (11%)
  other arithmetic  4.41 us (5%)
  local copies, waits for them, and re-layouts  1 us (1%)
    pallas_call x4, Pallas kernels, chunk_call(): pl.pallas_call(functools.partial(chunk_kernel, scale, parts, len(lses), h...  31.6 us
    pallas_call x1, Pallas kernels, column_call(): pl.pallas_call(functools.partial(column_kernel, scale, [len(part) for par...  19.3 us
    ppermute x13, starting transfers between devices, moved(): return lax.ppermute(value, 'control', perm)  11.7 us
    ppermute x13, waiting for transfers between devices, moved(): return lax.ppermute(value, 'control', perm)  6.96 us
    ppermute x3, starting transfers between devices, body(): lax.ppermute(column, 'treated', [(s, s ^ flip) for s in range(size)])  3.55 us
    reduce_sum x1, other arithmetic, body(): jnp.sum(jnp.square(control_emb.astype(jnp.float32)), axis=1) * inverse  3.07 us
    ppermute x3, waiting for transfers between devices, body(): lax.ppermute(column, 'treated', [(s, s ^ flip) for s in range(size)])  2.07 us
  transfers between devices with their start and end apart: 16, of which 10 were waited for; matrix products, arithmetic and copies ran while one was open for 5% of the time, Pallas kernels for 30%

profile of v2, /device:TPU:0, one launch (start us, length us, event | category | flops | bytes accessed | tf_op | source)
XLA Modules:
  0.0 82.6 jit_solution(16356068247974480069)
XLA Ops:
  0.6 0.0 copy-start
  0.6 0.0 copy-start.4
  0.6 0.5 collective-permute-start.1
  1.2 2.6 %collective-permute-start = (bf16[128,1024]{1,0:T(8,128)(2,1)}, bf16[128,1024]{1,0:T(8,128)(2,1)S(1)}, u32[]{:S(2)}, u32[]{:S(2)}) collective-permute-start(bf16[128,1024]{1,0:T(8,128)(2,1)} %refs_0_.2), channel_id=1, source_target_pairs={{0,2},{1,3},{2,4},{3,5},{4,6},{5,7},{6,0},{7,1},{8,10},{9,11},{10,... | collective-permute-start | bytes 786440 | tf_op jit(solution)/shard_map/ppermute | solution.py:342
  3.8 3.1 %multiply_reduce_fusion = f32[2048]{0:T(1024)S(1)} fusion(bf16[2048,1024]{1,0:T(8,128)(2,1)} %refs_22_.1), kind=kLoop, calls=%fused_computation | loop fusion | flops 6289408 | bytes 4202496 | tf_op jit(solution)/shard_map/reduce_sum | solution.py:334
  6.9 0.0 copy-done.4
  6.9 0.7 subtract_multiply_fusion
  7.6 2.2 %collective-permute-start.3 = (bf16[128,1024]{1,0:T(8,128)(2,1)}, bf16[128,1024]{1,0:T(8,128)(2,1)S(1)}, u32[]{:S(2)}, u32[]{:S(2)}) collective-permute-start(bf16[128,1024]{1,0:T(8,128)(2,1)} %refs_0_.2), channel_id=1, source_target_pairs={{0,6},{1,7},{2,0},{3,1},{4,2},{5,3},{6,4},{7,5},{8,14},{9,15},{10,... | collective-permute-start | bytes 786440 | tf_op jit(solution)/shard_map/ppermute | solution.py:342
  9.8 0.0 collective-permute-done.1.refs_1_.refs_9_
  9.8 0.0 copy-done
  9.8 0.0 copy-start.1
  9.8 1.0 %copy-done.1 = bf16[128,1024]{1,0:T(8,128)(2,1)S(1)} copy-done((bf16[128,1024]{1,0:T(8,128)(2,1)S(1)}, bf16[128,1024]{1,0:T(8,128)(2,1)}, u32[]{:S(2)}) %copy-start.1) | copy-done | bytes 262168
  10.8 7.9 %chunk_scores.4 = (f32[256,2048]{1,0:T(8,128)S(1)}, f32[2,128]{1,0:T(2,128)S(1)}, f32[2,128]{1,0:T(2,128)S(1)}) custom-call(bf16[128,1024]{1,0:T(8,128)(2,1)S(1)} %copy-done.1, bf16[128,1024]{1,0:T(8,128)(2,1)S(1)} %collective-permute-done.1.refs_1_.refs_9_, bf16[2048,1024]{1,0:T(8,128)(2,1)S(1)} %copy-done, f32[1,2048]{1,0:T(1,128)S(1)} %bitcast.5), custom_call_target="tpu_custom_call" | custom-call | flops 1073741824 | bytes 6815744 | tf_op jit(solution)/shard_map/chunk_scores/pallas_call | solution.py:123
  18.7 0.0 collective-permute-done.refs_0_.refs_10_.refs_2_
  18.7 0.2 collective-permute-start.4
  18.9 0.4 collective-permute-start.5
  19.3 0.0 collective-permute-start.2
  19.3 0.8 %collective-permute-done.4.refs_1_.refs_11_.refs_3_ = bf16[64,1024]{1,0:T(8,128)(2,1)S(1)} collective-permute-done((bf16[64,1024]{1,0:T(8,128)(2,1)S(1)}, bf16[64,1024]{1,0:T(8,128)(2,1)S(1)}, u32[]{:S(2)}, u32[]{:S(2)}) %collective-permute-start.4) | collective-permute-done | bytes 131104 | tf_op jit(solution)/shard_map/ppermute | solution.py:342
  20.1 0.2 collective-permute-done.5.refs_2_.refs_12_.refs_4_
  20.3 7.9 %chunk_scores.5 = (f32[256,2048]{1,0:T(8,128)S(1)}, f32[2,128]{1,0:T(2,128)S(1)}, f32[2,128]{1,0:T(2,128)S(1)}) custom-call(bf16[128,1024]{1,0:T(8,128)(2,1)S(1)} %collective-permute-done.refs_0_.refs_10_.refs_2_, bf16[64,1024]{1,0:T(8,128)(2,1)S(1)} %collective-permute-done.4.refs_1_.refs_11_.refs_3_, ...), custom_call_target="tpu_custom_call" | custom-call | tf_op jit(solution)/shard_map/chunk_scores/pallas_call | solution.py:123
  28.2 0.0 collective-permute-done.3.refs_0_.refs_13_.refs_5_
  28.2 0.1 collective-permute-start.6
  28.3 0.0 copy-start.3
  28.3 0.0 copy-start.2
  28.3 0.5 collective-permute-start.7
  28.8 0.8 %collective-permute-done.6.refs_1_.refs_14_.refs_6_ = bf16[64,1024]{1,0:T(8,128)(2,1)S(1)} collective-permute-done((bf16[64,1024]{1,0:T(8,128)(2,1)S(1)}, bf16[64,1024]{1,0:T(8,128)(2,1)S(1)}, u32[]{:S(2)}, u32[]{:S(2)}) %collective-permute-start.6) | collective-permute-done | bytes 131104 | tf_op jit(solution)/shard_map/ppermute | solution.py:342
  29.7 0.2 collective-permute-done.7.refs_2_.refs_15_.refs_7_
  29.8 7.9 %chunk_scores.6 = (f32[256,2048]{1,0:T(8,128)S(1)}, f32[2,128]{1,0:T(2,128)S(1)}, f32[2,128]{1,0:T(2,128)S(1)}) custom-call(bf16[128,1024]{1,0:T(8,128)(2,1)S(1)} %collective-permute-done.3.refs_0_.refs_13_.refs_5_, bf16[64,1024]{1,0:T(8,128)(2,1)S(1)} %collective-permute-done.6.refs_1_.refs_14_.refs_6_, ...), custom_call_target="tpu_custom_call" | custom-call | tf_op jit(solution)/shard_map/chunk_scores/pallas_call | solution.py:123
  37.7 0.0 collective-permute-done.2.refs_0_.refs_16_.refs_8_
  37.7 0.4 collective-permute-start.8
  38.1 1.2 %collective-permute-done.8.refs_1_.refs_17_.refs_9_ = bf16[128,1024]{1,0:T(8,128)(2,1)S(1)} collective-permute-done((bf16[128,1024]{1,0:T(8,128)(2,1)S(1)}, bf16[128,1024]{1,0:T(8,128)(2,1)S(1)}, u32[]{:S(2)}, u32[]{:S(2)}) %collective-permute-start.8) | collective-permute-done | bytes 262176 | tf_op jit(solution)/shard_map/ppermute | solution.py:342
  39.3 8.0 %chunk_scores.7 = (f32[256,2048]{1,0:T(8,128)S(1)}, f32[2,128]{1,0:T(2,128)S(1)}, f32[8,128]{1,0:T(8,128)S(1)}) custom-call(bf16[128,1024]{1,0:T(8,128)(2,1)S(1)} %collective-permute-done.2.refs_0_.refs_16_.refs_8_, bf16[128,1024]{1,0:T(8,128)(2,1)S(1)} %collective-permute-done.8.refs_1_.refs_17_.refs_9_, bf16[2048,1024]{1,0:T(8,128)(2,1)S(1)} %copy-done, ...), custom_call_target="tpu_custom_call" | custom-call | flops 1073741824 | bytes 6815744 | tf_op jit(solution)/shard_map/chunk_scores/pallas_call | solution.py:123
  47.3 0.4 collective-permute-start.9
  47.7 0.9 %collective-permute-done.9.second_ref = f32[8,128]{1,0:T(8,128)S(1)} collective-permute-done((f32[8,128]{1,0:T(8,128)S(1)}, f32[8,128]{1,0:T(8,128)S(1)}, u32[]{:S(2)}, u32[]{:S(2)}) %collective-permute-start.9) | collective-permute-done | bytes 4128 | tf_op jit(solution)/shard_map/ppermute | solution.py:342
  48.6 2.9 %collective-permute-start.12 = (f32[8,128]{1,0:T(8,128)S(1)}, f32[8,128]{1,0:T(8,128)S(1)}, u32[]{:S(2)}, u32[]{:S(2)}) collective-permute-start(f32[8,128]{1,0:T(8,128)S(1)} %merge_rows.1.refs_4_.refs_0_), channel_id=1, source_target_pairs={{0,6},{1,7},{2,4},{3,5},{4,2},{5,3},{6,0},{7,1},{8,14},{9,15},{10,... | collective-permute-start | bytes 12296 | tf_op jit(solution)/shard_map/ppermute | solution.py:342
  51.5 0.0 collective-permute-start.11
  51.5 1.6 %collective-permute-start.10 = (f32[8,128]{1,0:T(8,128)S(1)}, f32[8,128]{1,0:T(8,128)S(1)}, u32[]{:S(2)}, u32[]{:S(2)}) collective-permute-start(f32[8,128]{1,0:T(8,128)S(1)} %merge_rows.1.refs_4_.refs_0_), channel_id=1, source_target_pairs={{0,2},{1,3},{2,0},{3,1},{4,6},{5,7},{6,4},{7,5},{8,10},{9,11},{10,... | collective-permute-start | bytes 12296 | tf_op jit(solution)/shard_map/ppermute | solution.py:342
  53.0 0.0 copy-done.3
  53.0 0.1 row_weights.1
  53.1 0.9 %collective-permute-done.12.refs_3_ = f32[8,128]{1,0:T(8,128)S(1)} collective-permute-done((f32[8,128]{1,0:T(8,128)S(1)}, f32[8,128]{1,0:T(8,128)S(1)}, u32[]{:S(2)}, u32[]{:S(2)}) %collective-permute-start.12) | collective-permute-done | bytes 4128 | tf_op jit(solution)/shard_map/ppermute | solution.py:342
  54.1 1.9 %collective-permute-done.11.refs_2_ = f32[8,128]{1,0:T(8,128)S(1)} collective-permute-done((f32[8,128]{1,0:T(8,128)S(1)}, f32[8,128]{1,0:T(8,128)S(1)}, u32[]{:S(2)}, u32[]{:S(2)}) %collective-permute-start.11) | collective-permute-done | bytes 4128 | tf_op jit(solution)/shard_map/ppermute | solution.py:342
  56.0 0.0 collective-permute-done.10.refs_1_
  56.0 0.0 copy-done.2
  56.0 19.3 %column_lse.1 = (f32[16,128]{1,0:T(8,128)S(1)}, f32[8,128]{1,0:T(8,128)S(1)}) custom-call(f32[8,128]{1,0:T(8,128)S(1)} %merge_rows.1.refs_4_.refs_0_, f32[8,128]{1,0:T(8,128)S(1)} %collective-permute-done.10.refs_1_, f32[8,128]{1,0:T(8,128)S(1)} %collective-permute-done.11.refs_2_, f32[8,128]{1,0:T(8,128)S(1)} %collective-permute-done.12.refs_3_, ...), custom_call_target="tpu_custom_call" | custom-call | flops 4194304 | bytes 8388608 | tf_op jit(solution)/shard_map/column_lse/pallas_call | solution.py:280
  75.3 2.6 %collective-permute-start.15 = (f32[16,128]{1,0:T(8,128)S(1)}, f32[16,128]{1,0:T(8,128)S(1)}, u32[]{:S(2)}, u32[]{:S(2)}) collective-permute-start(f32[16,128]{1,0:T(8,128)S(1)} %get-tuple-element.77), channel_id=1, source_target_pairs={{0,24},{8,16},{16,8},{24,0},{1,25},{9,17},{17,9},{25,1},{2,26},{10... | collective-permute-start | bytes 24584 | tf_op jit(solution)/shard_map/ppermute | solution.py:398
  77.9 0.5 collective-permute-start.14
  78.3 0.5 collective-permute-start.13
  78.8 1.1 %treated_pot.1 = f32[8,128]{1,0:T(8,128)} custom-call(f32[8,128]{1,0:T(8,128)S(1)} %get-tuple-element.76.total_ref, bf16[128,1024]{1,0:T(8,128)(2,1)S(1)} %copy-done.2, bf16[128,1024]{1,0:T(8,128)(2,1)S(1)} %collective-permute-done.1.refs_1_.refs_9_, bf16[128,1024]{1,0:T(8,128)(2,1)S(1)} %collective-permute-done.refs_0_.refs_10_.refs_2_, ...), custom_call_target="tpu_custom_call" | custom-call | flops 2097152 | bytes 2097152 | tf_op jit(solution)/shard_map/treated_pot/pallas_call | solution.py:316
  79.9 0.0 collective-permute-done.15
  79.9 1.6 %collective-permute-done.14 = f32[16,128]{1,0:T(8,128)S(1)} collective-permute-done((f32[16,128]{1,0:T(8,128)S(1)}, f32[16,128]{1,0:T(8,128)S(1)}, u32[]{:S(2)}, u32[]{:S(2)}) %collective-permute-start.14) | collective-permute-done | bytes 8224 | tf_op jit(solution)/shard_map/ppermute | solution.py:398
  81.5 0.5 collective-permute-done.13
  82.0 0.6 bitcast_subtract_fusion
  (3 shorter events, 0.0 us)
Async XLA Ops:
  0.6 9.2 %copy-start = (bf16[2048,1024]{1,0:T(8,128)(2,1)S(1)}, bf16[2048,1024]{1,0:T(8,128)(2,1)}, u32[]{:S(2)}) copy-start(bf16[2048,1024]{1,0:T(8,128)(2,1)} %refs_22_.1) | copy-start | bytes 12582916
  0.6 6.2 %copy-start.4 = (f32[2048]{0:T(1024)S(1)}, f32[2048]{0:T(1024)}, u32[]{:S(2)}) copy-start(f32[2048]{0:T(1024)} %param.7) | copy-start | bytes 24580
  0.6 9.1 %collective-permute-start.1 = (bf16[128,1024]{1,0:T(8,128)(2,1)}, bf16[128,1024]{1,0:T(8,128)(2,1)S(1)}, u32[]{:S(2)}, u32[]{:S(2)}) collective-permute-start(bf16[128,1024]{1,0:T(8,128)(2,1)} %refs_0_.2), channel_id=1, source_target_pairs={{0,1},{1,0},{2,3},{3,2},{4,5},{5,4},{6,7},{7,6},{8,9},{9,8},{10,11... | collective-permute-start | bytes 786440 | tf_op jit(solution)/shard_map/ppermute | solution.py:342
  1.2 17.5 %collective-permute-start = (bf16[128,1024]{1,0:T(8,128)(2,1)}, bf16[128,1024]{1,0:T(8,128)(2,1)S(1)}, u32[]{:S(2)}, u32[]{:S(2)}) collective-permute-start(bf16[128,1024]{1,0:T(8,128)(2,1)} %refs_0_.2), channel_id=1, source_target_pairs={{0,2},{1,3},{2,4},{3,5},{4,6},{5,7},{6,0},{7,1},{8,10},{9,11},{10,... | collective-permute-start | bytes 786440 | tf_op jit(solution)/shard_map/ppermute | solution.py:342
  7.6 20.6 %collective-permute-start.3 = (bf16[128,1024]{1,0:T(8,128)(2,1)}, bf16[128,1024]{1,0:T(8,128)(2,1)S(1)}, u32[]{:S(2)}, u32[]{:S(2)}) collective-permute-start(bf16[128,1024]{1,0:T(8,128)(2,1)} %refs_0_.2), channel_id=1, source_target_pairs={{0,6},{1,7},{2,0},{3,1},{4,2},{5,3},{6,4},{7,5},{8,14},{9,15},{10,... | collective-permute-start | bytes 786440 | tf_op jit(solution)/shard_map/ppermute | solution.py:342
  9.8 1.0 %copy-start.1 = (bf16[128,1024]{1,0:T(8,128)(2,1)S(1)}, bf16[128,1024]{1,0:T(8,128)(2,1)}, u32[]{:S(2)}) copy-start(bf16[128,1024]{1,0:T(8,128)(2,1)} %refs_0_.2) | copy-start | bytes 786436
  18.7 1.4 %collective-permute-start.4 = (bf16[64,1024]{1,0:T(8,128)(2,1)S(1)}, bf16[64,1024]{1,0:T(8,128)(2,1)S(1)}, u32[]{:S(2)}, u32[]{:S(2)}) collective-permute-start(bf16[64,1024]{1,0:T(8,128)(2,1)S(1)} %get-tuple-element.44), channel_id=1, source_target_pairs={{0,1},{1,0},{2,3},{3,2},{4,5},{5,4},{6,7},{7,6},{8,9},{9,8},{10,11... | collective-permute-start | bytes 393224 | tf_op jit(solution)/shard_map/ppermute | solution.py:342
  18.9 1.4 %collective-permute-start.5 = (bf16[64,1024]{1,0:T(8,128)(2,1)S(1)}, bf16[64,1024]{1,0:T(8,128)(2,1)S(1)}, u32[]{:S(2)}, u32[]{:S(2)}) collective-permute-start(bf16[64,1024]{1,0:T(8,128)(2,1)S(1)} %get-tuple-element.45), channel_id=1, source_target_pairs={{0,1},{1,0},{2,3},{3,2},{4,5},{5,4},{6,7},{7,6},{8,9},{9,8},{10,11... | collective-permute-start | bytes 393224 | tf_op jit(solution)/shard_map/ppermute | solution.py:342
  19.3 18.4 %collective-permute-start.2 = (bf16[128,1024]{1,0:T(8,128)(2,1)S(1)}, bf16[128,1024]{1,0:T(8,128)(2,1)S(1)}, u32[]{:S(2)}, u32[]{:S(2)}) collective-permute-start(bf16[128,1024]{1,0:T(8,128)(2,1)S(1)} %collective-permute-done.refs_0_.refs_10_.refs_2_), channel_id=1, source_target_pairs={{0,2},{1,3},{2,4},{3,5},{4,6},{5,7},{6,0},{7,1},{8,10},{9,11},{10,... | collective-permute-start | bytes 786440 | tf_op jit(solution)/shard_map/ppermute | solution.py:342
  28.2 1.4 %collective-permute-start.6 = (bf16[64,1024]{1,0:T(8,128)(2,1)S(1)}, bf16[64,1024]{1,0:T(8,128)(2,1)S(1)}, u32[]{:S(2)}, u32[]{:S(2)}) collective-permute-start(bf16[64,1024]{1,0:T(8,128)(2,1)S(1)} %get-tuple-element.48), channel_id=1, source_target_pairs={{0,1},{1,0},{2,3},{3,2},{4,5},{5,4},{6,7},{7,6},{8,9},{9,8},{10,11... | collective-permute-start | bytes 393224 | tf_op jit(solution)/shard_map/ppermute | solution.py:342
  28.3 24.7 %copy-start.3 = (f32[1024]{0:T(1024)S(1)}, f32[1024]{0:T(1024)}, u32[]{:S(2)}) copy-start(f32[1024]{0:T(1024)} %param.9) | copy-start | bytes 12292
  28.3 27.6 %copy-start.2 = (bf16[128,1024]{1,0:T(8,128)(2,1)S(1)}, bf16[128,1024]{1,0:T(8,128)(2,1)}, u32[]{:S(2)}) copy-start(bf16[128,1024]{1,0:T(8,128)(2,1)} %refs_0_.2) | copy-start | bytes 786436
  28.3 1.5 %collective-permute-start.7 = (bf16[64,1024]{1,0:T(8,128)(2,1)S(1)}, bf16[64,1024]{1,0:T(8,128)(2,1)S(1)}, u32[]{:S(2)}, u32[]{:S(2)}) collective-permute-start(bf16[64,1024]{1,0:T(8,128)(2,1)S(1)} %get-tuple-element.49), channel_id=1, source_target_pairs={{0,1},{1,0},{2,3},{3,2},{4,5},{5,4},{6,7},{7,6},{8,9},{9,8},{10,11... | collective-permute-start | bytes 393224 | tf_op jit(solution)/shard_map/ppermute | solution.py:342
  37.7 1.6 %collective-permute-start.8 = (bf16[128,1024]{1,0:T(8,128)(2,1)S(1)}, bf16[128,1024]{1,0:T(8,128)(2,1)S(1)}, u32[]{:S(2)}, u32[]{:S(2)}) collective-permute-start(bf16[128,1024]{1,0:T(8,128)(2,1)S(1)} %collective-permute-done.2.refs_0_.refs_16_.refs_8_), channel_id=1, source_target_pairs={{0,1},{1,0},{2,3},{3,2},{4,5},{5,4},{6,7},{7,6},{8,9},{9,8},{10,11... | collective-permute-start | bytes 786440 | tf_op jit(solution)/shard_map/ppermute | solution.py:342
  47.3 1.2 %collective-permute-start.9 = (f32[8,128]{1,0:T(8,128)S(1)}, f32[8,128]{1,0:T(8,128)S(1)}, u32[]{:S(2)}, u32[]{:S(2)}) collective-permute-start(f32[8,128]{1,0:T(8,128)S(1)} %get-tuple-element.55.first_ref), channel_id=1, source_target_pairs={{0,1},{1,0},{2,3},{3,2},{4,5},{5,4},{6,7},{7,6},{8,9},{9,8},{10,11... | collective-permute-start | bytes 12296 | tf_op jit(solution)/shard_map/ppermute | solution.py:342
  48.6 5.5 %collective-permute-start.12 = (f32[8,128]{1,0:T(8,128)S(1)}, f32[8,128]{1,0:T(8,128)S(1)}, u32[]{:S(2)}, u32[]{:S(2)}) collective-permute-start(f32[8,128]{1,0:T(8,128)S(1)} %merge_rows.1.refs_4_.refs_0_), channel_id=1, source_target_pairs={{0,6},{1,7},{2,4},{3,5},{4,2},{5,3},{6,0},{7,1},{8,14},{9,15},{10,... | collective-permute-start | bytes 12296 | tf_op jit(solution)/shard_map/ppermute | solution.py:342
  51.5 4.5 %collective-permute-start.11 = (f32[8,128]{1,0:T(8,128)S(1)}, f32[8,128]{1,0:T(8,128)S(1)}, u32[]{:S(2)}, u32[]{:S(2)}) collective-permute-start(f32[8,128]{1,0:T(8,128)S(1)} %merge_rows.1.refs_4_.refs_0_), channel_id=1, source_target_pairs={{0,4},{1,5},{2,6},{3,7},{4,0},{5,1},{6,2},{7,3},{8,12},{9,13},{10,... | collective-permute-start | bytes 12296 | tf_op jit(solution)/shard_map/ppermute | solution.py:342
  51.5 4.5 %collective-permute-start.10 = (f32[8,128]{1,0:T(8,128)S(1)}, f32[8,128]{1,0:T(8,128)S(1)}, u32[]{:S(2)}, u32[]{:S(2)}) collective-permute-start(f32[8,128]{1,0:T(8,128)S(1)} %merge_rows.1.refs_4_.refs_0_), channel_id=1, source_target_pairs={{0,2},{1,3},{2,0},{3,1},{4,6},{5,7},{6,4},{7,5},{8,10},{9,11},{10,... | collective-permute-start | bytes 12296 | tf_op jit(solution)/shard_map/ppermute | solution.py:342
  75.3 4.6 %collective-permute-start.15 = (f32[16,128]{1,0:T(8,128)S(1)}, f32[16,128]{1,0:T(8,128)S(1)}, u32[]{:S(2)}, u32[]{:S(2)}) collective-permute-start(f32[16,128]{1,0:T(8,128)S(1)} %get-tuple-element.77), channel_id=1, source_target_pairs={{0,24},{8,16},{16,8},{24,0},{1,25},{9,17},{17,9},{25,1},{2,26},{10... | collective-permute-start | bytes 24584 | tf_op jit(solution)/shard_map/ppermute | solution.py:398
  77.9 3.7 %collective-permute-start.14 = (f32[16,128]{1,0:T(8,128)S(1)}, f32[16,128]{1,0:T(8,128)S(1)}, u32[]{:S(2)}, u32[]{:S(2)}) collective-permute-start(f32[16,128]{1,0:T(8,128)S(1)} %get-tuple-element.77), channel_id=1, source_target_pairs={{0,16},{8,24},{16,0},{24,8},{1,17},{9,25},{17,1},{25,9},{2,18},{10... | collective-permute-start | bytes 24584 | tf_op jit(solution)/shard_map/ppermute | solution.py:398
  78.3 3.7 %collective-permute-start.13 = (f32[16,128]{1,0:T(8,128)S(1)}, f32[16,128]{1,0:T(8,128)S(1)}, u32[]{:S(2)}, u32[]{:S(2)}) collective-permute-start(f32[16,128]{1,0:T(8,128)S(1)} %get-tuple-element.77), channel_id=1, source_target_pairs={{0,8},{8,0},{16,24},{24,16},{1,9},{9,1},{17,25},{25,17},{2,10},{10... | collective-permute-start | bytes 24584 | tf_op jit(solution)/shard_map/ppermute | solution.py:398

commit v3 on v2

--- a/solution.py
+++ b/solution.py
@@ -351,10 +351,11 @@
         held = (chips, ((0, 0), (0, 1), (1, 0), (1, 1), (3, 0), (3, 1), (2, 0), (2, 1)))
         x0 = treated_emb
         x1 = shifted(x0, 1)
-        p0 = swapped(x0)
+        behind, control_sq = lax.optimization_barrier((x0, control_sq))
+        p0 = [swapped(part) for part in halves_call([behind])]
         behind, u = lax.optimization_barrier((x0, u))
         x3 = shifted(behind, 3)
-        e0, top0, lse0 = chunk_call([x0, p0], control_emb, u)
+        e0, top0, lse0 = chunk_call([x0, *p0], control_emb, u)
         x1, lse0 = lax.optimization_barrier((x1, lse0))
         x2 = shifted(x1, 1)
         p1 = [swapped(part) for part in halves_call([x1])]
@@ -366,7 +367,7 @@
         p2 = swapped(x2)
         e3, top3, stats = chunk_call([x2, p2], control_emb, u, held, [lse0, lse1, lse2])
         exps, tops = [e0, e1, e2, e3], [top0, top1, top2, top3]
-        pieces = [x0, p0, x1, *p1, x3, *p3, x2, p2]
+        pieces = [x0, *p0, x1, *p1, x3, *p3, x2, p2]
         chip_stats = merge_call(stats, swapped(stats))
         stats = [chip_stats]
         for flip in (1, 2, 3):

time: 82.9 us -> 83.6 us (level)
  Pallas kernels: 52.2 us -> 53.2 us
  local copies, waits for them, and re-layouts: 1 us -> 0.01 us
    pallas_call x1, Pallas kernels: 19.3 us -> 20.4 us  [column_call(): pl.pallas_call(functools.partial(column_kernel, scale, [len(part) for par...]
    unnamed x10 -> x6, local copies, waits for them, and re-layouts: 1 us -> 0.01 us
    ppermute x13 -> x14, starting transfers between devices: 11.7 us -> 12.1 us  [moved(): return lax.ppermute(value, 'control', perm)]
    ppermute x13 -> x14, waiting for transfers between devices: 6.96 us -> 6.63 us  [moved(): return lax.ppermute(value, 'control', perm)]
  transfers between devices with their start and end apart: 16 -> 17, of which waited for: 10 -> 10; matrix products, arithmetic and copies ran while one was open for 5% -> 5% of each run, Pallas kernels for 30% -> 30%
where the time goes in v3:
time: 83.6 us; the launch traced here: 83.4 us
  Pallas kernels  53.2 us (64%)
  starting transfers between devices  15.9 us (19%)
  waiting for transfers between devices  9.08 us (11%)
  other arithmetic  4.42 us (5%)
    pallas_call x4, Pallas kernels, chunk_call(): pl.pallas_call(functools.partial(chunk_kernel, scale, parts, len(lses), h...  31.6 us
    pallas_call x1, Pallas kernels, column_call(): pl.pallas_call(functools.partial(column_kernel, scale, [len(part) for par...  20.4 us
    ppermute x14, starting transfers between devices, moved(): return lax.ppermute(value, 'control', perm)  12.1 us
    ppermute x14, waiting for transfers between devices, moved(): return lax.ppermute(value, 'control', perm)  6.63 us
    ppermute x3, starting transfers between devices, body(): lax.ppermute(column, 'treated', [(s, s ^ flip) for s in range(size)])  3.72 us
    reduce_sum x1, other arithmetic, body(): jnp.sum(jnp.square(control_emb.astype(jnp.float32)), axis=1) * inverse  3.07 us
    ppermute x3, waiting for transfers between devices, body(): lax.ppermute(column, 'treated', [(s, s ^ flip) for s in range(size)])  2.45 us
  transfers between devices with their start and end apart: 17, of which 10 were waited for; matrix products, arithmetic and copies ran while one was open for 5% of the time, Pallas kernels for 30%

profile of v3, /device:TPU:0, one launch (start us, length us, event | category | flops | bytes accessed | tf_op | source)
XLA Modules:
  0.0 83.4 jit_solution(13188659833125225210)
XLA Ops:
  0.6 0.0 copy-start.1
  0.6 0.0 copy-start
  0.6 3.1 %collective-permute-start = (bf16[128,1024]{1,0:T(8,128)(2,1)}, bf16[128,1024]{1,0:T(8,128)(2,1)S(1)}, u32[]{:S(2)}, u32[]{:S(2)}) collective-permute-start(bf16[128,1024]{1,0:T(8,128)(2,1)} %refs_0_.3), channel_id=1, source_target_pairs={{0,2},{1,3},{2,4},{3,5},{4,6},{5,7},{6,0},{7,1},{8,10},{9,11},{10,... | collective-permute-start | bytes 786440 | tf_op jit(solution)/shard_map/ppermute | solution.py:342
  3.7 3.1 %multiply_reduce_fusion = f32[2048]{0:T(1024)S(1)} fusion(bf16[2048,1024]{1,0:T(8,128)(2,1)} %refs_23_.1), kind=kLoop, calls=%fused_computation | loop fusion | flops 6289408 | bytes 4202496 | tf_op jit(solution)/shard_map/reduce_sum | solution.py:334
  6.8 0.7 subtract_multiply_fusion
  7.5 0.0 copy-done.1
  7.6 0.1 collective-permute-start.1
  7.6 0.5 collective-permute-start.2
  8.1 2.2 %collective-permute-start.4 = (bf16[128,1024]{1,0:T(8,128)(2,1)S(1)}, bf16[128,1024]{1,0:T(8,128)(2,1)S(1)}, u32[]{:S(2)}, u32[]{:S(2)}) collective-permute-start(bf16[128,1024]{1,0:T(8,128)(2,1)S(1)} %copy-done.1), channel_id=1, source_target_pairs={{0,6},{1,7},{2,0},{3,1},{4,2},{5,3},{6,4},{7,5},{8,14},{9,15},{10,... | collective-permute-start | bytes 786440 | tf_op jit(solution)/shard_map/ppermute | solution.py:342
  10.3 0.0 collective-permute-done.1.refs_1_.refs_9_
  10.3 0.0 collective-permute-done.2.refs_2_.refs_10_
  10.3 0.0 copy-done
  10.3 7.9 %chunk_scores.4 = (f32[256,2048]{1,0:T(8,128)S(1)}, f32[2,128]{1,0:T(2,128)S(1)}, f32[2,128]{1,0:T(2,128)S(1)}) custom-call(bf16[128,1024]{1,0:T(8,128)(2,1)S(1)} %copy-done.1, bf16[64,1024]{1,0:T(8,128)(2,1)S(1)} %collective-permute-done.1.refs_1_.refs_9_, bf16[64,1024]{1,0:T(8,128)(2,1)S(1)} %collective-permute-done.2.refs_2_.refs_10_, ...), custom_call_target="tpu_custom_call" | custom-call | flops 1073741824 | bytes 6815744 | tf_op jit(solution)/shard_map/chunk_scores/pallas_call | solution.py:123
  18.2 0.0 collective-permute-done.refs_0_.refs_11_.refs_3_
  18.3 0.1 collective-permute-start.5
  18.3 0.5 collective-permute-start.6
  18.8 0.4 collective-permute-start.3
  19.2 0.4 collective-permute-done.5.refs_1_.refs_12_.refs_4_
  19.7 0.2 collective-permute-done.6.refs_2_.refs_13_.refs_5_
  19.9 7.9 %chunk_scores.5 = (f32[256,2048]{1,0:T(8,128)S(1)}, f32[2,128]{1,0:T(2,128)S(1)}, f32[2,128]{1,0:T(2,128)S(1)}) custom-call(bf16[128,1024]{1,0:T(8,128)(2,1)S(1)} %collective-permute-done.refs_0_.refs_11_.refs_3_, bf16[64,1024]{1,0:T(8,128)(2,1)S(1)} %collective-permute-done.5.refs_1_.refs_12_.refs_4_, ...), custom_call_target="tpu_custom_call" | custom-call | tf_op jit(solution)/shard_map/chunk_scores/pallas_call | solution.py:123
  27.7 0.0 collective-permute-done.4.refs_0_.refs_14_.refs_6_
  27.8 0.4 collective-permute-start.7
  28.2 0.0 copy-start.2
  28.2 0.2 collective-permute-start.8
  28.4 0.8 %collective-permute-done.7.refs_1_.refs_15_.refs_7_ = bf16[64,1024]{1,0:T(8,128)(2,1)S(1)} collective-permute-done((bf16[64,1024]{1,0:T(8,128)(2,1)S(1)}, bf16[64,1024]{1,0:T(8,128)(2,1)S(1)}, u32[]{:S(2)}, u32[]{:S(2)}) %collective-permute-start.7) | collective-permute-done | bytes 131104 | tf_op jit(solution)/shard_map/ppermute | solution.py:342
  29.2 0.3 collective-permute-done.8.refs_2_.refs_16_.refs_8_
  29.5 7.9 %chunk_scores.6 = (f32[256,2048]{1,0:T(8,128)S(1)}, f32[2,128]{1,0:T(2,128)S(1)}, f32[2,128]{1,0:T(2,128)S(1)}) custom-call(bf16[128,1024]{1,0:T(8,128)(2,1)S(1)} %collective-permute-done.4.refs_0_.refs_14_.refs_6_, bf16[64,1024]{1,0:T(8,128)(2,1)S(1)} %collective-permute-done.7.refs_1_.refs_15_.refs_7_, ...), custom_call_target="tpu_custom_call" | custom-call | tf_op jit(solution)/shard_map/chunk_scores/pallas_call | solution.py:123
  37.4 0.0 collective-permute-done.3.refs_0_.refs_17_.refs_9_
  37.4 0.2 collective-permute-start.9
  37.7 1.4 %collective-permute-done.9.refs_1_.refs_18_.refs_10_ = bf16[128,1024]{1,0:T(8,128)(2,1)S(1)} collective-permute-done((bf16[128,1024]{1,0:T(8,128)(2,1)S(1)}, bf16[128,1024]{1,0:T(8,128)(2,1)S(1)}, u32[]{:S(2)}, u32[]{:S(2)}) %collective-permute-start.9) | collective-permute-done | bytes 262176 | tf_op jit(solution)/shard_map/ppermute | solution.py:342
  39.0 7.9 %chunk_scores.7 = (f32[256,2048]{1,0:T(8,128)S(1)}, f32[2,128]{1,0:T(2,128)S(1)}, f32[8,128]{1,0:T(8,128)S(1)}) custom-call(bf16[128,1024]{1,0:T(8,128)(2,1)S(1)} %collective-permute-done.3.refs_0_.refs_17_.refs_9_, bf16[128,1024]{1,0:T(8,128)(2,1)S(1)} %collective-permute-done.9.refs_1_.refs_18_.refs_10_, bf16[2048,1024]{1,0:T(8,128)(2,1)S(1)} %copy-done, ...), custom_call_target="tpu_custom_call" | custom-call | flops 1073741824 | bytes 6815744 | tf_op jit(solution)/shard_map/chunk_scores/pallas_call | solution.py:123
  47.0 0.1 collective-permute-start.10
  47.0 1.2 %collective-permute-done.10.second_ref = f32[8,128]{1,0:T(8,128)S(1)} collective-permute-done((f32[8,128]{1,0:T(8,128)S(1)}, f32[8,128]{1,0:T(8,128)S(1)}, u32[]{:S(2)}, u32[]{:S(2)}) %collective-permute-start.10) | collective-permute-done | bytes 4128 | tf_op jit(solution)/shard_map/ppermute | solution.py:342
  48.2 2.4 %collective-permute-start.13 = (f32[8,128]{1,0:T(8,128)S(1)}, f32[8,128]{1,0:T(8,128)S(1)}, u32[]{:S(2)}, u32[]{:S(2)}) collective-permute-start(f32[8,128]{1,0:T(8,128)S(1)} %merge_rows.1.refs_4_.refs_0_), channel_id=1, source_target_pairs={{0,6},{1,7},{2,4},{3,5},{4,2},{5,3},{6,0},{7,1},{8,14},{9,15},{10,... | collective-permute-start | bytes 12296 | tf_op jit(solution)/shard_map/ppermute | solution.py:342
  50.6 0.0 collective-permute-start.12
  50.6 2.1 %collective-permute-start.11 = (f32[8,128]{1,0:T(8,128)S(1)}, f32[8,128]{1,0:T(8,128)S(1)}, u32[]{:S(2)}, u32[]{:S(2)}) collective-permute-start(f32[8,128]{1,0:T(8,128)S(1)} %merge_rows.1.refs_4_.refs_0_), channel_id=1, source_target_pairs={{0,2},{1,3},{2,0},{3,1},{4,6},{5,7},{6,4},{7,5},{8,10},{9,11},{10,... | collective-permute-start | bytes 12296 | tf_op jit(solution)/shard_map/ppermute | solution.py:342
  52.7 0.0 copy-done.2
  52.7 0.1 row_weights.1
  52.8 0.9 %collective-permute-done.13.refs_3_ = f32[8,128]{1,0:T(8,128)S(1)} collective-permute-done((f32[8,128]{1,0:T(8,128)S(1)}, f32[8,128]{1,0:T(8,128)S(1)}, u32[]{:S(2)}, u32[]{:S(2)}) %collective-permute-start.13) | collective-permute-done | bytes 4128 | tf_op jit(solution)/shard_map/ppermute | solution.py:342
  53.7 1.4 %collective-permute-done.12.refs_2_ = f32[8,128]{1,0:T(8,128)S(1)} collective-permute-done((f32[8,128]{1,0:T(8,128)S(1)}, f32[8,128]{1,0:T(8,128)S(1)}, u32[]{:S(2)}, u32[]{:S(2)}) %collective-permute-start.12) | collective-permute-done | bytes 4128 | tf_op jit(solution)/shard_map/ppermute | solution.py:342
  55.1 0.0 collective-permute-done.11.refs_1_
  55.1 20.4 %column_lse.1 = (f32[16,128]{1,0:T(8,128)S(1)}, f32[8,128]{1,0:T(8,128)S(1)}) custom-call(f32[8,128]{1,0:T(8,128)S(1)} %merge_rows.1.refs_4_.refs_0_, f32[8,128]{1,0:T(8,128)S(1)} %collective-permute-done.11.refs_1_, f32[8,128]{1,0:T(8,128)S(1)} %collective-permute-done.12.refs_2_, f32[8,128]{1,0:T(8,128)S(1)} %collective-permute-done.13.refs_3_, ...), custom_call_target="tpu_custom_call" | custom-call | flops 4194304 | bytes 8388608 | tf_op jit(solution)/shard_map/column_lse/pallas_call | solution.py:280
  75.5 3.1 %collective-permute-start.16 = (f32[16,128]{1,0:T(8,128)S(1)}, f32[16,128]{1,0:T(8,128)S(1)}, u32[]{:S(2)}, u32[]{:S(2)}) collective-permute-start(f32[16,128]{1,0:T(8,128)S(1)} %get-tuple-element.86), channel_id=1, source_target_pairs={{0,24},{8,16},{16,8},{24,0},{1,25},{9,17},{17,9},{25,1},{2,26},{10... | collective-permute-start | bytes 24584 | tf_op jit(solution)/shard_map/ppermute | solution.py:399
  78.6 0.5 collective-permute-start.15
  79.1 0.1 collective-permute-start.14
  79.2 1.1 %treated_pot.1 = f32[8,128]{1,0:T(8,128)} custom-call(f32[8,128]{1,0:T(8,128)S(1)} %get-tuple-element.85.total_ref, bf16[128,1024]{1,0:T(8,128)(2,1)S(1)} %copy-done.1, bf16[64,1024]{1,0:T(8,128)(2,1)S(1)} %collective-permute-done.1.refs_1_.refs_9_, bf16[64,1024]{1,0:T(8,128)(2,1)S(1)} %collective-permute-done.2.refs_2_.refs_10_, ...), custom_call_target="tpu_custom_call" | custom-call | flops 2097152 | bytes 2097152 | tf_op jit(solution)/shard_map/treated_pot/pallas_call | solution.py:316
  80.3 0.0 collective-permute-done.16
  80.3 1.9 %collective-permute-done.15 = f32[16,128]{1,0:T(8,128)S(1)} collective-permute-done((f32[16,128]{1,0:T(8,128)S(1)}, f32[16,128]{1,0:T(8,128)S(1)}, u32[]{:S(2)}, u32[]{:S(2)}) %collective-permute-start.15) | collective-permute-done | bytes 8224 | tf_op jit(solution)/shard_map/ppermute | solution.py:399
  82.2 0.5 collective-permute-done.14
  82.7 0.6 bitcast_subtract_fusion
  (4 shorter events, 0.1 us)
Async XLA Ops:
  0.6 6.9 %copy-start.1 = (bf16[128,1024]{1,0:T(8,128)(2,1)S(1)}, bf16[128,1024]{1,0:T(8,128)(2,1)}, u32[]{:S(2)}) copy-start(bf16[128,1024]{1,0:T(8,128)(2,1)} %refs_0_.3) | copy-start | bytes 786436
  0.6 9.7 %copy-start = (bf16[2048,1024]{1,0:T(8,128)(2,1)S(1)}, bf16[2048,1024]{1,0:T(8,128)(2,1)}, u32[]{:S(2)}) copy-start(bf16[2048,1024]{1,0:T(8,128)(2,1)} %refs_23_.1) | copy-start | bytes 12582916
  0.6 17.6 %collective-permute-start = (bf16[128,1024]{1,0:T(8,128)(2,1)}, bf16[128,1024]{1,0:T(8,128)(2,1)S(1)}, u32[]{:S(2)}, u32[]{:S(2)}) collective-permute-start(bf16[128,1024]{1,0:T(8,128)(2,1)} %refs_0_.3), channel_id=1, source_target_pairs={{0,2},{1,3},{2,4},{3,5},{4,6},{5,7},{6,0},{7,1},{8,10},{9,11},{10,... | collective-permute-start | bytes 786440 | tf_op jit(solution)/shard_map/ppermute | solution.py:342
  7.6 2.8 %collective-permute-start.1 = (bf16[64,1024]{1,0:T(8,128)(2,1)S(1)}, bf16[64,1024]{1,0:T(8,128)(2,1)S(1)}, u32[]{:S(2)}, u32[]{:S(2)}) collective-permute-start(bf16[64,1024]{1,0:T(8,128)(2,1)S(1)} %get-tuple-element.46), channel_id=1, source_target_pairs={{0,1},{1,0},{2,3},{3,2},{4,5},{5,4},{6,7},{7,6},{8,9},{9,8},{10,11... | collective-permute-start | bytes 393224 | tf_op jit(solution)/shard_map/ppermute | solution.py:342
  7.6 2.7 %collective-permute-start.2 = (bf16[64,1024]{1,0:T(8,128)(2,1)S(1)}, bf16[64,1024]{1,0:T(8,128)(2,1)S(1)}, u32[]{:S(2)}, u32[]{:S(2)}) collective-permute-start(bf16[64,1024]{1,0:T(8,128)(2,1)S(1)} %get-tuple-element.47), channel_id=1, source_target_pairs={{0,1},{1,0},{2,3},{3,2},{4,5},{5,4},{6,7},{7,6},{8,9},{9,8},{10,11... | collective-permute-start | bytes 393224 | tf_op jit(solution)/shard_map/ppermute | solution.py:342
  8.1 19.6 %collective-permute-start.4 = (bf16[128,1024]{1,0:T(8,128)(2,1)S(1)}, bf16[128,1024]{1,0:T(8,128)(2,1)S(1)}, u32[]{:S(2)}, u32[]{:S(2)}) collective-permute-start(bf16[128,1024]{1,0:T(8,128)(2,1)S(1)} %copy-done.1), channel_id=1, source_target_pairs={{0,6},{1,7},{2,0},{3,1},{4,2},{5,3},{6,4},{7,5},{8,14},{9,15},{10,... | collective-permute-start | bytes 786440 | tf_op jit(solution)/shard_map/ppermute | solution.py:342
  18.3 1.4 %collective-permute-start.5 = (bf16[64,1024]{1,0:T(8,128)(2,1)S(1)}, bf16[64,1024]{1,0:T(8,128)(2,1)S(1)}, u32[]{:S(2)}, u32[]{:S(2)}) collective-permute-start(bf16[64,1024]{1,0:T(8,128)(2,1)S(1)} %get-tuple-element.52), channel_id=1, source_target_pairs={{0,1},{1,0},{2,3},{3,2},{4,5},{5,4},{6,7},{7,6},{8,9},{9,8},{10,11... | collective-permute-start | bytes 393224 | tf_op jit(solution)/shard_map/ppermute | solution.py:342
  18.3 1.5 %collective-permute-start.6 = (bf16[64,1024]{1,0:T(8,128)(2,1)S(1)}, bf16[64,1024]{1,0:T(8,128)(2,1)S(1)}, u32[]{:S(2)}, u32[]{:S(2)}) collective-permute-start(bf16[64,1024]{1,0:T(8,128)(2,1)S(1)} %get-tuple-element.53), channel_id=1, source_target_pairs={{0,1},{1,0},{2,3},{3,2},{4,5},{5,4},{6,7},{7,6},{8,9},{9,8},{10,11... | collective-permute-start | bytes 393224 | tf_op jit(solution)/shard_map/ppermute | solution.py:342
  18.8 18.6 %collective-permute-start.3 = (bf16[128,1024]{1,0:T(8,128)(2,1)S(1)}, bf16[128,1024]{1,0:T(8,128)(2,1)S(1)}, u32[]{:S(2)}, u32[]{:S(2)}) collective-permute-start(bf16[128,1024]{1,0:T(8,128)(2,1)S(1)} %collective-permute-done.refs_0_.refs_11_.refs_3_), channel_id=1, source_target_pairs={{0,2},{1,3},{2,4},{3,5},{4,6},{5,7},{6,0},{7,1},{8,10},{9,11},{10,... | collective-permute-start | bytes 786440 | tf_op jit(solution)/shard_map/ppermute | solution.py:342
  27.8 1.4 %collective-permute-start.7 = (bf16[64,1024]{1,0:T(8,128)(2,1)S(1)}, bf16[64,1024]{1,0:T(8,128)(2,1)S(1)}, u32[]{:S(2)}, u32[]{:S(2)}) collective-permute-start(bf16[64,1024]{1,0:T(8,128)(2,1)S(1)} %get-tuple-element.56), channel_id=1, source_target_pairs={{0,1},{1,0},{2,3},{3,2},{4,5},{5,4},{6,7},{7,6},{8,9},{9,8},{10,11... | collective-permute-start | bytes 393224 | tf_op jit(solution)/shard_map/ppermute | solution.py:342
  28.2 24.5 %copy-start.2 = (f32[1024]{0:T(1024)S(1)}, f32[1024]{0:T(1024)}, u32[]{:S(2)}) copy-start(f32[1024]{0:T(1024)} %param.9) | copy-start | bytes 12292
  28.2 1.3 %collective-permute-start.8 = (bf16[64,1024]{1,0:T(8,128)(2,1)S(1)}, bf16[64,1024]{1,0:T(8,128)(2,1)S(1)}, u32[]{:S(2)}, u32[]{:S(2)}) collective-permute-start(bf16[64,1024]{1,0:T(8,128)(2,1)S(1)} %get-tuple-element.57), channel_id=1, source_target_pairs={{0,1},{1,0},{2,3},{3,2},{4,5},{5,4},{6,7},{7,6},{8,9},{9,8},{10,11... | collective-permute-start | bytes 393224 | tf_op jit(solution)/shard_map/ppermute | solution.py:342
  37.4 1.6 %collective-permute-start.9 = (bf16[128,1024]{1,0:T(8,128)(2,1)S(1)}, bf16[128,1024]{1,0:T(8,128)(2,1)S(1)}, u32[]{:S(2)}, u32[]{:S(2)}) collective-permute-start(bf16[128,1024]{1,0:T(8,128)(2,1)S(1)} %collective-permute-done.3.refs_0_.refs_17_.refs_9_), channel_id=1, source_target_pairs={{0,1},{1,0},{2,3},{3,2},{4,5},{5,4},{6,7},{7,6},{8,9},{9,8},{10,11... | collective-permute-start | bytes 786440 | tf_op jit(solution)/shard_map/ppermute | solution.py:342
  47.0 1.2 %collective-permute-start.10 = (f32[8,128]{1,0:T(8,128)S(1)}, f32[8,128]{1,0:T(8,128)S(1)}, u32[]{:S(2)}, u32[]{:S(2)}) collective-permute-start(f32[8,128]{1,0:T(8,128)S(1)} %get-tuple-element.63.first_ref), channel_id=1, source_target_pairs={{0,1},{1,0},{2,3},{3,2},{4,5},{5,4},{6,7},{7,6},{8,9},{9,8},{10,11... | collective-permute-start | bytes 12296 | tf_op jit(solution)/shard_map/ppermute | solution.py:342
  48.2 5.5 %collective-permute-start.13 = (f32[8,128]{1,0:T(8,128)S(1)}, f32[8,128]{1,0:T(8,128)S(1)}, u32[]{:S(2)}, u32[]{:S(2)}) collective-permute-start(f32[8,128]{1,0:T(8,128)S(1)} %merge_rows.1.refs_4_.refs_0_), channel_id=1, source_target_pairs={{0,6},{1,7},{2,4},{3,5},{4,2},{5,3},{6,0},{7,1},{8,14},{9,15},{10,... | collective-permute-start | bytes 12296 | tf_op jit(solution)/shard_map/ppermute | solution.py:342
  50.6 4.5 %collective-permute-start.12 = (f32[8,128]{1,0:T(8,128)S(1)}, f32[8,128]{1,0:T(8,128)S(1)}, u32[]{:S(2)}, u32[]{:S(2)}) collective-permute-start(f32[8,128]{1,0:T(8,128)S(1)} %merge_rows.1.refs_4_.refs_0_), channel_id=1, source_target_pairs={{0,4},{1,5},{2,6},{3,7},{4,0},{5,1},{6,2},{7,3},{8,12},{9,13},{10,... | collective-permute-start | bytes 12296 | tf_op jit(solution)/shard_map/ppermute | solution.py:342
  50.6 4.5 %collective-permute-start.11 = (f32[8,128]{1,0:T(8,128)S(1)}, f32[8,128]{1,0:T(8,128)S(1)}, u32[]{:S(2)}, u32[]{:S(2)}) collective-permute-start(f32[8,128]{1,0:T(8,128)S(1)} %merge_rows.1.refs_4_.refs_0_), channel_id=1, source_target_pairs={{0,2},{1,3},{2,0},{3,1},{4,6},{5,7},{6,4},{7,5},{8,10},{9,11},{10,... | collective-permute-start | bytes 12296 | tf_op jit(solution)/shard_map/ppermute | solution.py:342
  75.5 4.8 %collective-permute-start.16 = (f32[16,128]{1,0:T(8,128)S(1)}, f32[16,128]{1,0:T(8,128)S(1)}, u32[]{:S(2)}, u32[]{:S(2)}) collective-permute-start(f32[16,128]{1,0:T(8,128)S(1)} %get-tuple-element.86), channel_id=1, source_target_pairs={{0,24},{8,16},{16,8},{24,0},{1,25},{9,17},{17,9},{25,1},{2,26},{10... | collective-permute-start | bytes 24584 | tf_op jit(solution)/shard_map/ppermute | solution.py:399
  78.6 3.7 %collective-permute-start.15 = (f32[16,128]{1,0:T(8,128)S(1)}, f32[16,128]{1,0:T(8,128)S(1)}, u32[]{:S(2)}, u32[]{:S(2)}) collective-permute-start(f32[16,128]{1,0:T(8,128)S(1)} %get-tuple-element.86), channel_id=1, source_target_pairs={{0,16},{8,24},{16,0},{24,8},{1,17},{9,25},{17,1},{25,9},{2,18},{10... | collective-permute-start | bytes 24584 | tf_op jit(solution)/shard_map/ppermute | solution.py:399
  79.1 3.7 %collective-permute-start.14 = (f32[16,128]{1,0:T(8,128)S(1)}, f32[16,128]{1,0:T(8,128)S(1)}, u32[]{:S(2)}, u32[]{:S(2)}) collective-permute-start(f32[16,128]{1,0:T(8,128)S(1)} %get-tuple-element.86), channel_id=1, source_target_pairs={{0,8},{8,0},{16,24},{24,16},{1,9},{9,1},{17,25},{25,17},{2,10},{10... | collective-permute-start | bytes 24584 | tf_op jit(solution)/shard_map/ppermute | solution.py:399

commit v4 on v2

--- a/solution.py
+++ b/solution.py
@@ -162,6 +162,23 @@
 
 def merge_kernel(first_ref, second_ref, out_ref):
     out_ref[...] = log2_sum([first_ref[...], second_ref[...]])
+
+
+def share_kernel(own_ref, near_ref, far_ref, out_ref):
+    far = far_ref[...]
+    out_ref[...] = jnp.where(lax.axis_index("control") % 2 == 0, log2_sum([own_ref[...], near_ref[...], far]), far)
+
+
+def share_call(own, near, far):
+    return pl.pallas_call(
+        share_kernel,
+        in_specs=[WHOLE] * 3,
+        out_specs=WHOLE,
+        out_shape=jax.ShapeDtypeStruct(own.shape, jnp.float32),
+        compiler_params=params(1),
+        cost_estimate=pl.CostEstimate(flops=8 * own.size, bytes_accessed=16 * own.size, transcendentals=0),
+        name="share_rows",
+    )(own, near, far)
 
 
 def merge_call(first, second):
@@ -368,9 +385,10 @@
         exps, tops = [e0, e1, e2, e3], [top0, top1, top2, top3]
         pieces = [x0, p0, x1, *p1, x3, *p3, x2, p2]
         chip_stats = merge_call(stats, swapped(stats))
-        stats = [chip_stats]
-        for flip in (1, 2, 3):
-            stats.append(moved(chip_stats, lambda z, c: (z ^ flip) * 2 + c))
+        near = moved(chip_stats, lambda z, c: (z ^ 1) * 2 + c)
+        far = moved(chip_stats, lambda z, c: (z ^ (2 + c)) * 2 + c)
+        share = share_call(chip_stats, near, far)
+        stats, bound = [share, swapped(share)], chip_stats
     else:
         held = None
         block = lax.all_gather(treated_emb, "control", axis=0, tiled=True)
@@ -384,10 +402,11 @@
         gathered = lax.all_gather(jnp.concatenate(lses, axis=0), "control")
         top = jnp.max(gathered, axis=0)
         stats = [top + jnp.log2(jnp.sum(jnp.exp2(gathered - top[None]), axis=0))]
+        bound = stats[0]
 
     if ring:
         pieces = list(lax.optimization_barrier((tuple(pieces), stats[-1]))[0])
-    base, most = weight_call(held, tops, stats[0], logw)
+    base, most = weight_call(held, tops, bound, logw)
     column, total = column_call(held, stats, exps, pieces, base, most, logw, u, control_emb)
     treated_pot = pot_call(held, total, pieces, inverse).reshape(-1)
 

time: 82.9 us -> 81.6 us (0.984)
  starting transfers between devices: 15.2 us -> 14.1 us
    ppermute x13, starting transfers between devices: 11.7 us -> 10.6 us  [moved(): return lax.ppermute(value, 'control', perm)]
  transfers between devices with their start and end apart: 16 -> 16, of which waited for: 10 -> 11; matrix products, arithmetic and copies ran while one was open for 5% -> 5% of each run, Pallas kernels for 30% -> 31%
where the time goes in v4:
time: 81.6 us; the launch traced here: 81.4 us
  Pallas kernels  52.1 us (64%)
  starting transfers between devices  14.1 us (17%)
  waiting for transfers between devices  9.04 us (11%)
  other arithmetic  4.41 us (5%)
  local copies, waits for them, and re-layouts  0.99 us (1%)
    pallas_call x4, Pallas kernels, chunk_call(): pl.pallas_call(functools.partial(chunk_kernel, scale, parts, len(lses), h...  31.5 us
    pallas_call x1, Pallas kernels, column_call(): pl.pallas_call(functools.partial(column_kernel, scale, [len(part) for par...  19.3 us
    ppermute x13, starting transfers between devices, moved(): return lax.ppermute(value, 'control', perm)  10.6 us
    ppermute x13, waiting for transfers between devices, moved(): return lax.ppermute(value, 'control', perm)  6.98 us
    ppermute x3, starting transfers between devices, body(): lax.ppermute(column, 'treated', [(s, s ^ flip) for s in range(size)])  3.55 us
    reduce_sum x1, other arithmetic, body(): jnp.sum(jnp.square(control_emb.astype(jnp.float32)), axis=1) * inverse  3.07 us
    ppermute x3, waiting for transfers between devices, body(): lax.ppermute(column, 'treated', [(s, s ^ flip) for s in range(size)])  2.07 us
  transfers between devices with their start and end apart: 16, of which 11 were waited for; matrix products, arithmetic and copies ran while one was open for 5% of the time, Pallas kernels for 31%

profile of v4, /device:TPU:0, one launch (start us, length us, event | category | flops | bytes accessed | tf_op | source)
XLA Modules:
  0.0 81.4 jit_solution(11523125260603159637)
XLA Ops:
  0.6 0.0 copy-start
  0.6 0.0 copy-start.4
  0.6 0.5 collective-permute-start.1
  1.2 2.6 %collective-permute-start = (bf16[128,1024]{1,0:T(8,128)(2,1)}, bf16[128,1024]{1,0:T(8,128)(2,1)S(1)}, u32[]{:S(2)}, u32[]{:S(2)}) collective-permute-start(bf16[128,1024]{1,0:T(8,128)(2,1)} %refs_0_.2), channel_id=1, source_target_pairs={{0,2},{1,3},{2,4},{3,5},{4,6},{5,7},{6,0},{7,1},{8,10},{9,11},{10,... | collective-permute-start | bytes 786440 | tf_op jit(solution)/shard_map/ppermute | solution.py:359
  3.8 3.1 %multiply_reduce_fusion = f32[2048]{0:T(1024)S(1)} fusion(bf16[2048,1024]{1,0:T(8,128)(2,1)} %refs_20_.1), kind=kLoop, calls=%fused_computation | loop fusion | flops 6289408 | bytes 4202496 | tf_op jit(solution)/shard_map/reduce_sum | solution.py:351
  6.9 0.0 copy-done.4
  6.9 0.7 subtract_multiply_fusion
  7.6 2.2 %collective-permute-start.3 = (bf16[128,1024]{1,0:T(8,128)(2,1)}, bf16[128,1024]{1,0:T(8,128)(2,1)S(1)}, u32[]{:S(2)}, u32[]{:S(2)}) collective-permute-start(bf16[128,1024]{1,0:T(8,128)(2,1)} %refs_0_.2), channel_id=1, source_target_pairs={{0,6},{1,7},{2,0},{3,1},{4,2},{5,3},{6,4},{7,5},{8,14},{9,15},{10,... | collective-permute-start | bytes 786440 | tf_op jit(solution)/shard_map/ppermute | solution.py:359
  9.8 0.0 collective-permute-done.1.refs_1_.refs_7_
  9.8 0.0 copy-done
  9.8 0.0 copy-start.1
  9.8 1.0 %copy-done.1 = bf16[128,1024]{1,0:T(8,128)(2,1)S(1)} copy-done((bf16[128,1024]{1,0:T(8,128)(2,1)S(1)}, bf16[128,1024]{1,0:T(8,128)(2,1)}, u32[]{:S(2)}) %copy-start.1) | copy-done | bytes 262168
  10.8 7.9 %chunk_scores.4 = (f32[256,2048]{1,0:T(8,128)S(1)}, f32[2,128]{1,0:T(2,128)S(1)}, f32[2,128]{1,0:T(2,128)S(1)}) custom-call(bf16[128,1024]{1,0:T(8,128)(2,1)S(1)} %copy-done.1, bf16[128,1024]{1,0:T(8,128)(2,1)S(1)} %collective-permute-done.1.refs_1_.refs_7_, bf16[2048,1024]{1,0:T(8,128)(2,1)S(1)} %copy-done, f32[1,2048]{1,0:T(1,128)S(1)} %bitcast.5), custom_call_target="tpu_custom_call" | custom-call | flops 1073741824 | bytes 6815744 | tf_op jit(solution)/shard_map/chunk_scores/pallas_call | solution.py:123
  18.7 0.0 collective-permute-done.refs_0_.refs_8_.refs_2_
  18.7 0.2 collective-permute-start.4
  18.9 0.4 collective-permute-start.5
  19.3 0.0 collective-permute-start.2
  19.3 0.8 %collective-permute-done.4.refs_1_.refs_9_.refs_3_ = bf16[64,1024]{1,0:T(8,128)(2,1)S(1)} collective-permute-done((bf16[64,1024]{1,0:T(8,128)(2,1)S(1)}, bf16[64,1024]{1,0:T(8,128)(2,1)S(1)}, u32[]{:S(2)}, u32[]{:S(2)}) %collective-permute-start.4) | collective-permute-done | bytes 131104 | tf_op jit(solution)/shard_map/ppermute | solution.py:359
  20.1 0.2 collective-permute-done.5.refs_2_.refs_10_.refs_4_
  20.3 7.9 %chunk_scores.5 = (f32[256,2048]{1,0:T(8,128)S(1)}, f32[2,128]{1,0:T(2,128)S(1)}, f32[2,128]{1,0:T(2,128)S(1)}) custom-call(bf16[128,1024]{1,0:T(8,128)(2,1)S(1)} %collective-permute-done.refs_0_.refs_8_.refs_2_, bf16[64,1024]{1,0:T(8,128)(2,1)S(1)} %collective-permute-done.4.refs_1_.refs_9_.refs_3_, ...), custom_call_target="tpu_custom_call" | custom-call | tf_op jit(solution)/shard_map/chunk_scores/pallas_call | solution.py:123
  28.2 0.0 collective-permute-done.3.refs_0_.refs_11_.refs_5_
  28.2 0.4 collective-permute-start.6
  28.6 0.0 copy-start.3
  28.6 0.0 copy-start.2
  28.6 0.2 collective-permute-start.7
  28.8 0.8 %collective-permute-done.6.refs_1_.refs_12_.refs_6_ = bf16[64,1024]{1,0:T(8,128)(2,1)S(1)} collective-permute-done((bf16[64,1024]{1,0:T(8,128)(2,1)S(1)}, bf16[64,1024]{1,0:T(8,128)(2,1)S(1)}, u32[]{:S(2)}, u32[]{:S(2)}) %collective-permute-start.6) | collective-permute-done | bytes 131104 | tf_op jit(solution)/shard_map/ppermute | solution.py:359
  29.6 0.3 collective-permute-done.7.refs_2_.refs_13_.refs_7_
  29.9 7.9 %chunk_scores.6 = (f32[256,2048]{1,0:T(8,128)S(1)}, f32[2,128]{1,0:T(2,128)S(1)}, f32[2,128]{1,0:T(2,128)S(1)}) custom-call(bf16[128,1024]{1,0:T(8,128)(2,1)S(1)} %collective-permute-done.3.refs_0_.refs_11_.refs_5_, bf16[64,1024]{1,0:T(8,128)(2,1)S(1)} %collective-permute-done.6.refs_1_.refs_12_.refs_6_, ...), custom_call_target="tpu_custom_call" | custom-call | tf_op jit(solution)/shard_map/chunk_scores/pallas_call | solution.py:123
  37.8 0.0 collective-permute-done.2.refs_0_.refs_14_.refs_8_
  37.8 0.3 collective-permute-start.8
  38.1 1.3 %collective-permute-done.8.refs_1_.refs_15_.refs_9_ = bf16[128,1024]{1,0:T(8,128)(2,1)S(1)} collective-permute-done((bf16[128,1024]{1,0:T(8,128)(2,1)S(1)}, bf16[128,1024]{1,0:T(8,128)(2,1)S(1)}, u32[]{:S(2)}, u32[]{:S(2)}) %collective-permute-start.8) | collective-permute-done | bytes 262176 | tf_op jit(solution)/shard_map/ppermute | solution.py:359
  39.4 7.9 %chunk_scores.7 = (f32[256,2048]{1,0:T(8,128)S(1)}, f32[2,128]{1,0:T(2,128)S(1)}, f32[8,128]{1,0:T(8,128)S(1)}) custom-call(bf16[128,1024]{1,0:T(8,128)(2,1)S(1)} %collective-permute-done.2.refs_0_.refs_14_.refs_8_, bf16[128,1024]{1,0:T(8,128)(2,1)S(1)} %collective-permute-done.8.refs_1_.refs_15_.refs_9_, bf16[2048,1024]{1,0:T(8,128)(2,1)S(1)} %copy-done, ...), custom_call_target="tpu_custom_call" | custom-call | flops 1073741824 | bytes 6815744 | tf_op jit(solution)/shard_map/chunk_scores/pallas_call | solution.py:123
  47.3 0.1 collective-permute-start.9
  47.4 1.2 %collective-permute-done.9.second_ref = f32[8,128]{1,0:T(8,128)S(1)} collective-permute-done((f32[8,128]{1,0:T(8,128)S(1)}, f32[8,128]{1,0:T(8,128)S(1)}, u32[]{:S(2)}, u32[]{:S(2)}) %collective-permute-start.9) | collective-permute-done | bytes 4128 | tf_op jit(solution)/shard_map/ppermute | solution.py:359
  48.6 1.3 %collective-permute-start.11 = (f32[8,128]{1,0:T(8,128)S(1)}, f32[8,128]{1,0:T(8,128)S(1)}, u32[]{:S(2)}, u32[]{:S(2)}) collective-permute-start(f32[8,128]{1,0:T(8,128)S(1)} %merge_rows.1.own_ref.refs_4_), channel_id=1, source_target_pairs={{0,4},{1,7},{2,6},{3,5},{4,0},{5,3},{6,2},{7,1},{8,12},{9,15},{10,... | collective-permute-start | bytes 12296 | tf_op jit(solution)/shard_map/ppermute | solution.py:359
  49.9 2.0 %collective-permute-start.10 = (f32[8,128]{1,0:T(8,128)S(1)}, f32[8,128]{1,0:T(8,128)S(1)}, u32[]{:S(2)}, u32[]{:S(2)}) collective-permute-start(f32[8,128]{1,0:T(8,128)S(1)} %merge_rows.1.own_ref.refs_4_), channel_id=1, source_target_pairs={{0,2},{1,3},{2,0},{3,1},{4,6},{5,7},{6,4},{7,5},{8,10},{9,11},{10,... | collective-permute-start | bytes 12296 | tf_op jit(solution)/shard_map/ppermute | solution.py:359
  51.9 1.2 %collective-permute-done.11.far_ref = f32[8,128]{1,0:T(8,128)S(1)} collective-permute-done((f32[8,128]{1,0:T(8,128)S(1)}, f32[8,128]{1,0:T(8,128)S(1)}, u32[]{:S(2)}, u32[]{:S(2)}) %collective-permute-start.11) | collective-permute-done | bytes 4128 | tf_op jit(solution)/shard_map/ppermute | solution.py:359
  53.2 0.4 collective-permute-done.10.near_ref
  53.5 0.4 collective-permute-start.12
  53.9 0.0 copy-done.3
  53.9 0.1 row_weights.1
  54.0 0.7 collective-permute-done.12.refs_1_
  54.8 0.0 copy-done.2
  54.8 19.3 %column_lse.1 = (f32[16,128]{1,0:T(8,128)S(1)}, f32[8,128]{1,0:T(8,128)S(1)}) custom-call(f32[8,128]{1,0:T(8,128)S(1)} %share_rows.1.refs_0_, f32[8,128]{1,0:T(8,128)S(1)} %collective-permute-done.12.refs_1_, f32[256,2048]{1,0:T(8,128)S(1)} %get-tuple-element.56.refs_2_, f32[256,2048]{1,0:T(8,128)S(1)} %get-tuple-element.57.refs_3_, ...), custom_call_target="tpu_custom_call" | custom-call | flops 4194304 | bytes 8388608 | tf_op jit(solution)/shard_map/column_lse/pallas_call | solution.py:297
  74.1 2.5 %collective-permute-start.15 = (f32[16,128]{1,0:T(8,128)S(1)}, f32[16,128]{1,0:T(8,128)S(1)}, u32[]{:S(2)}, u32[]{:S(2)}) collective-permute-start(f32[16,128]{1,0:T(8,128)S(1)} %get-tuple-element.77), channel_id=1, source_target_pairs={{0,24},{8,16},{16,8},{24,0},{1,25},{9,17},{17,9},{25,1},{2,26},{10... | collective-permute-start | bytes 24584 | tf_op jit(solution)/shard_map/ppermute | solution.py:417
  76.6 0.5 collective-permute-start.14
  77.1 0.5 collective-permute-start.13
  77.6 1.1 %treated_pot.1 = f32[8,128]{1,0:T(8,128)} custom-call(f32[8,128]{1,0:T(8,128)S(1)} %get-tuple-element.76.total_ref, bf16[128,1024]{1,0:T(8,128)(2,1)S(1)} %copy-done.2, bf16[128,1024]{1,0:T(8,128)(2,1)S(1)} %collective-permute-done.1.refs_1_.refs_7_, bf16[128,1024]{1,0:T(8,128)(2,1)S(1)} %collective-permute-done.refs_0_.refs_8_.refs_2_, ...), custom_call_target="tpu_custom_call" | custom-call | flops 2097152 | bytes 2097152 | tf_op jit(solution)/shard_map/treated_pot/pallas_call | solution.py:333
  78.7 0.0 collective-permute-done.15
  78.7 1.5 %collective-permute-done.14 = f32[16,128]{1,0:T(8,128)S(1)} collective-permute-done((f32[16,128]{1,0:T(8,128)S(1)}, f32[16,128]{1,0:T(8,128)S(1)}, u32[]{:S(2)}, u32[]{:S(2)}) %collective-permute-start.14) | collective-permute-done | bytes 8224 | tf_op jit(solution)/shard_map/ppermute | solution.py:417
  80.3 0.5 collective-permute-done.13
  80.8 0.6 bitcast_subtract_fusion
  (4 shorter events, 0.1 us)
Async XLA Ops:
  0.6 9.2 %copy-start = (bf16[2048,1024]{1,0:T(8,128)(2,1)S(1)}, bf16[2048,1024]{1,0:T(8,128)(2,1)}, u32[]{:S(2)}) copy-start(bf16[2048,1024]{1,0:T(8,128)(2,1)} %refs_20_.1) | copy-start | bytes 12582916
  0.6 6.2 %copy-start.4 = (f32[2048]{0:T(1024)S(1)}, f32[2048]{0:T(1024)}, u32[]{:S(2)}) copy-start(f32[2048]{0:T(1024)} %param.7) | copy-start | bytes 24580
  0.6 9.1 %collective-permute-start.1 = (bf16[128,1024]{1,0:T(8,128)(2,1)}, bf16[128,1024]{1,0:T(8,128)(2,1)S(1)}, u32[]{:S(2)}, u32[]{:S(2)}) collective-permute-start(bf16[128,1024]{1,0:T(8,128)(2,1)} %refs_0_.2), channel_id=1, source_target_pairs={{0,1},{1,0},{2,3},{3,2},{4,5},{5,4},{6,7},{7,6},{8,9},{9,8},{10,11... | collective-permute-start | bytes 786440 | tf_op jit(solution)/shard_map/ppermute | solution.py:359
  1.2 17.5 %collective-permute-start = (bf16[128,1024]{1,0:T(8,128)(2,1)}, bf16[128,1024]{1,0:T(8,128)(2,1)S(1)}, u32[]{:S(2)}, u32[]{:S(2)}) collective-permute-start(bf16[128,1024]{1,0:T(8,128)(2,1)} %refs_0_.2), channel_id=1, source_target_pairs={{0,2},{1,3},{2,4},{3,5},{4,6},{5,7},{6,0},{7,1},{8,10},{9,11},{10,... | collective-permute-start | bytes 786440 | tf_op jit(solution)/shard_map/ppermute | solution.py:359
  7.6 20.6 %collective-permute-start.3 = (bf16[128,1024]{1,0:T(8,128)(2,1)}, bf16[128,1024]{1,0:T(8,128)(2,1)S(1)}, u32[]{:S(2)}, u32[]{:S(2)}) collective-permute-start(bf16[128,1024]{1,0:T(8,128)(2,1)} %refs_0_.2), channel_id=1, source_target_pairs={{0,6},{1,7},{2,0},{3,1},{4,2},{5,3},{6,4},{7,5},{8,14},{9,15},{10,... | collective-permute-start | bytes 786440 | tf_op jit(solution)/shard_map/ppermute | solution.py:359
  9.8 1.0 %copy-start.1 = (bf16[128,1024]{1,0:T(8,128)(2,1)S(1)}, bf16[128,1024]{1,0:T(8,128)(2,1)}, u32[]{:S(2)}) copy-start(bf16[128,1024]{1,0:T(8,128)(2,1)} %refs_0_.2) | copy-start | bytes 786436
  18.7 1.4 %collective-permute-start.4 = (bf16[64,1024]{1,0:T(8,128)(2,1)S(1)}, bf16[64,1024]{1,0:T(8,128)(2,1)S(1)}, u32[]{:S(2)}, u32[]{:S(2)}) collective-permute-start(bf16[64,1024]{1,0:T(8,128)(2,1)S(1)} %get-tuple-element.44), channel_id=1, source_target_pairs={{0,1},{1,0},{2,3},{3,2},{4,5},{5,4},{6,7},{7,6},{8,9},{9,8},{10,11... | collective-permute-start | bytes 393224 | tf_op jit(solution)/shard_map/ppermute | solution.py:359
  18.9 1.4 %collective-permute-start.5 = (bf16[64,1024]{1,0:T(8,128)(2,1)S(1)}, bf16[64,1024]{1,0:T(8,128)(2,1)S(1)}, u32[]{:S(2)}, u32[]{:S(2)}) collective-permute-start(bf16[64,1024]{1,0:T(8,128)(2,1)S(1)} %get-tuple-element.45), channel_id=1, source_target_pairs={{0,1},{1,0},{2,3},{3,2},{4,5},{5,4},{6,7},{7,6},{8,9},{9,8},{10,11... | collective-permute-start | bytes 393224 | tf_op jit(solution)/shard_map/ppermute | solution.py:359
  19.3 18.6 %collective-permute-start.2 = (bf16[128,1024]{1,0:T(8,128)(2,1)S(1)}, bf16[128,1024]{1,0:T(8,128)(2,1)S(1)}, u32[]{:S(2)}, u32[]{:S(2)}) collective-permute-start(bf16[128,1024]{1,0:T(8,128)(2,1)S(1)} %collective-permute-done.refs_0_.refs_8_.refs_2_), channel_id=1, source_target_pairs={{0,2},{1,3},{2,4},{3,5},{4,6},{5,7},{6,0},{7,1},{8,10},{9,11},{10,... | collective-permute-start | bytes 786440 | tf_op jit(solution)/shard_map/ppermute | solution.py:359
  28.2 1.4 %collective-permute-start.6 = (bf16[64,1024]{1,0:T(8,128)(2,1)S(1)}, bf16[64,1024]{1,0:T(8,128)(2,1)S(1)}, u32[]{:S(2)}, u32[]{:S(2)}) collective-permute-start(bf16[64,1024]{1,0:T(8,128)(2,1)S(1)} %get-tuple-element.48), channel_id=1, source_target_pairs={{0,1},{1,0},{2,3},{3,2},{4,5},{5,4},{6,7},{7,6},{8,9},{9,8},{10,11... | collective-permute-start | bytes 393224 | tf_op jit(solution)/shard_map/ppermute | solution.py:359
  28.6 25.3 %copy-start.3 = (f32[1024]{0:T(1024)S(1)}, f32[1024]{0:T(1024)}, u32[]{:S(2)}) copy-start(f32[1024]{0:T(1024)} %param.9) | copy-start | bytes 12292
  28.6 26.2 %copy-start.2 = (bf16[128,1024]{1,0:T(8,128)(2,1)S(1)}, bf16[128,1024]{1,0:T(8,128)(2,1)}, u32[]{:S(2)}) copy-start(bf16[128,1024]{1,0:T(8,128)(2,1)} %refs_0_.2) | copy-start | bytes 786436
  28.6 1.3 %collective-permute-start.7 = (bf16[64,1024]{1,0:T(8,128)(2,1)S(1)}, bf16[64,1024]{1,0:T(8,128)(2,1)S(1)}, u32[]{:S(2)}, u32[]{:S(2)}) collective-permute-start(bf16[64,1024]{1,0:T(8,128)(2,1)S(1)} %get-tuple-element.49), channel_id=1, source_target_pairs={{0,1},{1,0},{2,3},{3,2},{4,5},{5,4},{6,7},{7,6},{8,9},{9,8},{10,11... | collective-permute-start | bytes 393224 | tf_op jit(solution)/shard_map/ppermute | solution.py:359
  37.8 1.6 %collective-permute-start.8 = (bf16[128,1024]{1,0:T(8,128)(2,1)S(1)}, bf16[128,1024]{1,0:T(8,128)(2,1)S(1)}, u32[]{:S(2)}, u32[]{:S(2)}) collective-permute-start(bf16[128,1024]{1,0:T(8,128)(2,1)S(1)} %collective-permute-done.2.refs_0_.refs_14_.refs_8_), channel_id=1, source_target_pairs={{0,1},{1,0},{2,3},{3,2},{4,5},{5,4},{6,7},{7,6},{8,9},{9,8},{10,11... | collective-permute-start | bytes 786440 | tf_op jit(solution)/shard_map/ppermute | solution.py:359
  47.3 1.2 %collective-permute-start.9 = (f32[8,128]{1,0:T(8,128)S(1)}, f32[8,128]{1,0:T(8,128)S(1)}, u32[]{:S(2)}, u32[]{:S(2)}) collective-permute-start(f32[8,128]{1,0:T(8,128)S(1)} %get-tuple-element.55.first_ref), channel_id=1, source_target_pairs={{0,1},{1,0},{2,3},{3,2},{4,5},{5,4},{6,7},{7,6},{8,9},{9,8},{10,11... | collective-permute-start | bytes 12296 | tf_op jit(solution)/shard_map/ppermute | solution.py:359
  48.6 4.6 %collective-permute-start.11 = (f32[8,128]{1,0:T(8,128)S(1)}, f32[8,128]{1,0:T(8,128)S(1)}, u32[]{:S(2)}, u32[]{:S(2)}) collective-permute-start(f32[8,128]{1,0:T(8,128)S(1)} %merge_rows.1.own_ref.refs_4_), channel_id=1, source_target_pairs={{0,4},{1,7},{2,6},{3,5},{4,0},{5,3},{6,2},{7,1},{8,12},{9,15},{10,... | collective-permute-start | bytes 12296 | tf_op jit(solution)/shard_map/ppermute | solution.py:359
  49.9 3.6 %collective-permute-start.10 = (f32[8,128]{1,0:T(8,128)S(1)}, f32[8,128]{1,0:T(8,128)S(1)}, u32[]{:S(2)}, u32[]{:S(2)}) collective-permute-start(f32[8,128]{1,0:T(8,128)S(1)} %merge_rows.1.own_ref.refs_4_), channel_id=1, source_target_pairs={{0,2},{1,3},{2,0},{3,1},{4,6},{5,7},{6,4},{7,5},{8,10},{9,11},{10,... | collective-permute-start | bytes 12296 | tf_op jit(solution)/shard_map/ppermute | solution.py:359
  53.5 1.2 %collective-permute-start.12 = (f32[8,128]{1,0:T(8,128)S(1)}, f32[8,128]{1,0:T(8,128)S(1)}, u32[]{:S(2)}, u32[]{:S(2)}) collective-permute-start(f32[8,128]{1,0:T(8,128)S(1)} %share_rows.1.refs_0_), channel_id=1, source_target_pairs={{0,1},{1,0},{2,3},{3,2},{4,5},{5,4},{6,7},{7,6},{8,9},{9,8},{10,11... | collective-permute-start | bytes 12296 | tf_op jit(solution)/shard_map/ppermute | solution.py:359
  74.1 4.6 %collective-permute-start.15 = (f32[16,128]{1,0:T(8,128)S(1)}, f32[16,128]{1,0:T(8,128)S(1)}, u32[]{:S(2)}, u32[]{:S(2)}) collective-permute-start(f32[16,128]{1,0:T(8,128)S(1)} %get-tuple-element.77), channel_id=1, source_target_pairs={{0,24},{8,16},{16,8},{24,0},{1,25},{9,17},{17,9},{25,1},{2,26},{10... | collective-permute-start | bytes 24584 | tf_op jit(solution)/shard_map/ppermute | solution.py:417
  76.6 3.7 %collective-permute-start.14 = (f32[16,128]{1,0:T(8,128)S(1)}, f32[16,128]{1,0:T(8,128)S(1)}, u32[]{:S(2)}, u32[]{:S(2)}) collective-permute-start(f32[16,128]{1,0:T(8,128)S(1)} %get-tuple-element.77), channel_id=1, source_target_pairs={{0,16},{8,24},{16,0},{24,8},{1,17},{9,25},{17,1},{25,9},{2,18},{10... | collective-permute-start | bytes 24584 | tf_op jit(solution)/shard_map/ppermute | solution.py:417
  77.1 3.7 %collective-permute-start.13 = (f32[16,128]{1,0:T(8,128)S(1)}, f32[16,128]{1,0:T(8,128)S(1)}, u32[]{:S(2)}, u32[]{:S(2)}) collective-permute-start(f32[16,128]{1,0:T(8,128)S(1)} %get-tuple-element.77), channel_id=1, source_target_pairs={{0,8},{8,0},{16,24},{24,16},{1,9},{9,1},{17,25},{25,17},{2,10},{10... | collective-permute-start | bytes 24584 | tf_op jit(solution)/shard_map/ppermute | solution.py:417

commit v5 on v4

--- a/solution.py
+++ b/solution.py
@@ -164,12 +164,12 @@
     out_ref[...] = log2_sum([first_ref[...], second_ref[...]])
 
 
-def share_kernel(own_ref, near_ref, far_ref, out_ref):
-    far = far_ref[...]
-    out_ref[...] = jnp.where(lax.axis_index("control") % 2 == 0, log2_sum([own_ref[...], near_ref[...], far]), far)
-
-
-def share_call(own, near, far):
+def share_kernel(own_ref, first_ref, second_ref, out_ref):
+    other = jnp.where(lax.axis_index("control") % 2 == 0, own_ref[...], second_ref[...])
+    out_ref[...] = log2_sum([first_ref[...], other])
+
+
+def share_call(own, first, second):
     return pl.pallas_call(
         share_kernel,
         in_specs=[WHOLE] * 3,
@@ -178,7 +178,7 @@
         compiler_params=params(1),
         cost_estimate=pl.CostEstimate(flops=8 * own.size, bytes_accessed=16 * own.size, transcendentals=0),
         name="share_rows",
-    )(own, near, far)
+    )(own, first, second)
 
 
 def merge_call(first, second):
@@ -385,9 +385,9 @@
         exps, tops = [e0, e1, e2, e3], [top0, top1, top2, top3]
         pieces = [x0, p0, x1, *p1, x3, *p3, x2, p2]
         chip_stats = merge_call(stats, swapped(stats))
-        near = moved(chip_stats, lambda z, c: (z ^ 1) * 2 + c)
-        far = moved(chip_stats, lambda z, c: (z ^ (2 + c)) * 2 + c)
-        share = share_call(chip_stats, near, far)
+        second = moved(chip_stats, lambda z, c: (z ^ (1 + c)) * 2 + c)
+        first = moved(chip_stats, lambda z, c: (z ^ (1 + 2 * c)) * 2 + c)
+        share = share_call(chip_stats, first, second)
         stats, bound = [share, swapped(share)], chip_stats
     else:
         held = None

time: 81.6 us -> 81.7 us (level)
  Pallas kernels: 52.1 us -> 45.7 us
  starting transfers between devices: 14.1 us -> 19.2 us
  waiting for transfers between devices: 9.04 us -> 10.7 us
    pallas_call x4, Pallas kernels: 31.5 us -> 25.2 us  [chunk_call(): pl.pallas_call(functools.partial(chunk_kernel, scale, parts, len(lses), h...]
    ppermute x13, starting transfers between devices: 10.6 us -> 15.6 us  [moved(): return lax.ppermute(value, 'control', perm)]
    ppermute x13, waiting for transfers between devices: 6.98 us -> 8.67 us  [moved(): return lax.ppermute(value, 'control', perm)]
  transfers between devices with their start and end apart: 16 -> 16, of which waited for: 11 -> 11; matrix products, arithmetic and copies ran while one was open for 5% -> 5% of each run, Pallas kernels for 31% -> 30%
where the time goes in v5:
time: 81.7 us
  Pallas kernels  45.7 us (56%)
  starting transfers between devices  19.2 us (24%)
  waiting for transfers between devices  10.7 us (13%)
  other arithmetic  4.41 us (5%)
  local copies, waits for them, and re-layouts  0.99 us (1%)
    pallas_call x4, Pallas kernels, chunk_call(): pl.pallas_call(functools.partial(chunk_kernel, scale, parts, len(lses), h...  25.2 us
    pallas_call x1, Pallas kernels, column_call(): pl.pallas_call(functools.partial(column_kernel, scale, [len(part) for par...  19.3 us
    ppermute x13, starting transfers between devices, moved(): return lax.ppermute(value, 'control', perm)  15.6 us
    ppermute x13, waiting for transfers between devices, moved(): return lax.ppermute(value, 'control', perm)  8.67 us
    ppermute x3, starting transfers between devices, body(): lax.ppermute(column, 'treated', [(s, s ^ flip) for s in range(size)])  3.55 us
    reduce_sum x1, other arithmetic, body(): jnp.sum(jnp.square(control_emb.astype(jnp.float32)), axis=1) * inverse  3.07 us
    ppermute x3, waiting for transfers between devices, body(): lax.ppermute(column, 'treated', [(s, s ^ flip) for s in range(size)])  2.05 us
  transfers between devices with their start and end apart: 16, of which 11 were waited for; matrix products, arithmetic and copies ran while one was open for 5% of the time, Pallas kernels for 30%

profile of v5, /device:TPU:0, one launch (start us, length us, event | category | flops | bytes accessed | tf_op | source)
XLA Modules:
  0.0 81.7 jit_solution(12416601050119720390)
XLA Ops:
  0.6 0.0 copy-start
  0.6 0.0 copy-start.4
  0.6 0.5 collective-permute-start.1
  1.2 2.6 %collective-permute-start = (bf16[128,1024]{1,0:T(8,128)(2,1)}, bf16[128,1024]{1,0:T(8,128)(2,1)S(1)}, u32[]{:S(2)}, u32[]{:S(2)}) collective-permute-start(bf16[128,1024]{1,0:T(8,128)(2,1)} %refs_0_.2), channel_id=1, source_target_pairs={{0,2},{1,3},{2,4},{3,5},{4,6},{5,7},{6,0},{7,1},{8,10},{9,11},{10,... | collective-permute-start | bytes 786440 | tf_op jit(solution)/shard_map/ppermute | solution.py:359
  3.8 3.1 %multiply_reduce_fusion = f32[2048]{0:T(1024)S(1)} fusion(bf16[2048,1024]{1,0:T(8,128)(2,1)} %refs_20_.1), kind=kLoop, calls=%fused_computation | loop fusion | flops 6289408 | bytes 4202496 | tf_op jit(solution)/shard_map/reduce_sum | solution.py:351
  6.9 0.0 copy-done.4
  6.9 0.7 subtract_multiply_fusion
  7.6 2.2 %collective-permute-start.3 = (bf16[128,1024]{1,0:T(8,128)(2,1)}, bf16[128,1024]{1,0:T(8,128)(2,1)S(1)}, u32[]{:S(2)}, u32[]{:S(2)}) collective-permute-start(bf16[128,1024]{1,0:T(8,128)(2,1)} %refs_0_.2), channel_id=1, source_target_pairs={{0,6},{1,7},{2,0},{3,1},{4,2},{5,3},{6,4},{7,5},{8,14},{9,15},{10,... | collective-permute-start | bytes 786440 | tf_op jit(solution)/shard_map/ppermute | solution.py:359
  9.8 0.0 collective-permute-done.1.refs_1_.refs_7_
  9.8 0.0 copy-done
  9.8 0.0 copy-start.1
  9.8 1.0 %copy-done.1 = bf16[128,1024]{1,0:T(8,128)(2,1)S(1)} copy-done((bf16[128,1024]{1,0:T(8,128)(2,1)S(1)}, bf16[128,1024]{1,0:T(8,128)(2,1)}, u32[]{:S(2)}) %copy-start.1) | copy-done | bytes 262168
  10.8 7.9 %chunk_scores.4 = (f32[256,2048]{1,0:T(8,128)S(1)}, f32[2,128]{1,0:T(2,128)S(1)}, f32[2,128]{1,0:T(2,128)S(1)}) custom-call(bf16[128,1024]{1,0:T(8,128)(2,1)S(1)} %copy-done.1, bf16[128,1024]{1,0:T(8,128)(2,1)S(1)} %collective-permute-done.1.refs_1_.refs_7_, bf16[2048,1024]{1,0:T(8,128)(2,1)S(1)} %copy-done, f32[1,2048]{1,0:T(1,128)S(1)} %bitcast.5), custom_call_target="tpu_custom_call" | custom-call | flops 1073741824 | bytes 6815744 | tf_op jit(solution)/shard_map/chunk_scores/pallas_call | solution.py:123
  18.7 0.0 collective-permute-done.refs_0_.refs_8_.refs_2_
  18.7 0.2 collective-permute-start.4
  18.9 0.4 collective-permute-start.5
  19.3 0.0 collective-permute-start.2
  19.3 0.8 %collective-permute-done.4.refs_1_.refs_9_.refs_3_ = bf16[64,1024]{1,0:T(8,128)(2,1)S(1)} collective-permute-done((bf16[64,1024]{1,0:T(8,128)(2,1)S(1)}, bf16[64,1024]{1,0:T(8,128)(2,1)S(1)}, u32[]{:S(2)}, u32[]{:S(2)}) %collective-permute-start.4) | collective-permute-done | bytes 131104 | tf_op jit(solution)/shard_map/ppermute | solution.py:359
  20.1 0.2 collective-permute-done.5.refs_2_.refs_10_.refs_4_
  20.3 7.9 %chunk_scores.5 = (f32[256,2048]{1,0:T(8,128)S(1)}, f32[2,128]{1,0:T(2,128)S(1)}, f32[2,128]{1,0:T(2,128)S(1)}) custom-call(bf16[128,1024]{1,0:T(8,128)(2,1)S(1)} %collective-permute-done.refs_0_.refs_8_.refs_2_, bf16[64,1024]{1,0:T(8,128)(2,1)S(1)} %collective-permute-done.4.refs_1_.refs_9_.refs_3_, ...), custom_call_target="tpu_custom_call" | custom-call | tf_op jit(solution)/shard_map/chunk_scores/pallas_call | solution.py:123
  28.2 0.0 collective-permute-done.3.refs_0_.refs_11_.refs_5_
  28.2 0.4 collective-permute-start.6
  28.6 0.0 copy-start.3
  28.6 0.0 copy-start.2
  28.6 0.2 collective-permute-start.7
  28.8 0.8 %collective-permute-done.6.refs_1_.refs_12_.refs_6_ = bf16[64,1024]{1,0:T(8,128)(2,1)S(1)} collective-permute-done((bf16[64,1024]{1,0:T(8,128)(2,1)S(1)}, bf16[64,1024]{1,0:T(8,128)(2,1)S(1)}, u32[]{:S(2)}, u32[]{:S(2)}) %collective-permute-start.6) | collective-permute-done | bytes 131104 | tf_op jit(solution)/shard_map/ppermute | solution.py:359
  29.6 0.3 collective-permute-done.7.refs_2_.refs_13_.refs_7_
  29.9 7.9 %chunk_scores.6 = (f32[256,2048]{1,0:T(8,128)S(1)}, f32[2,128]{1,0:T(2,128)S(1)}, f32[2,128]{1,0:T(2,128)S(1)}) custom-call(bf16[128,1024]{1,0:T(8,128)(2,1)S(1)} %collective-permute-done.3.refs_0_.refs_11_.refs_5_, bf16[64,1024]{1,0:T(8,128)(2,1)S(1)} %collective-permute-done.6.refs_1_.refs_12_.refs_6_, ...), custom_call_target="tpu_custom_call" | custom-call | tf_op jit(solution)/shard_map/chunk_scores/pallas_call | solution.py:123
  37.8 0.0 collective-permute-done.2.refs_0_.refs_14_.refs_8_
  37.8 0.3 collective-permute-start.8
  38.1 1.3 %collective-permute-done.8.refs_1_.refs_15_.refs_9_ = bf16[128,1024]{1,0:T(8,128)(2,1)S(1)} collective-permute-done((bf16[128,1024]{1,0:T(8,128)(2,1)S(1)}, bf16[128,1024]{1,0:T(8,128)(2,1)S(1)}, u32[]{:S(2)}, u32[]{:S(2)}) %collective-permute-start.8) | collective-permute-done | bytes 262176 | tf_op jit(solution)/shard_map/ppermute | solution.py:359
  39.4 1.6 %chunk_scores.7 = (f32[256,2048]{1,0:T(8,128)S(1)}, f32[2,128]{1,0:T(2,128)S(1)}, f32[8,128]{1,0:T(8,128)S(1)}) custom-call(bf16[128,1024]{1,0:T(8,128)(2,1)S(1)} %collective-permute-done.2.refs_0_.refs_14_.refs_8_, bf16[128,1024]{1,0:T(8,128)(2,1)S(1)} %collective-permute-done.8.refs_1_.refs_15_.refs_9_, bf16[2048,1024]{1,0:T(8,128)(2,1)S(1)} %copy-done, ...), custom_call_target="tpu_custom_call" | custom-call | flops 1073741824 | bytes 6815744 | tf_op jit(solution)/shard_map/chunk_scores/pallas_call | solution.py:123
  41.0 0.3 collective-permute-start.9
  41.3 0.9 %collective-permute-done.9.second_ref = f32[8,128]{1,0:T(8,128)S(1)} collective-permute-done((f32[8,128]{1,0:T(8,128)S(1)}, f32[8,128]{1,0:T(8,128)S(1)}, u32[]{:S(2)}, u32[]{:S(2)}) %collective-permute-start.9) | collective-permute-done | bytes 4128 | tf_op jit(solution)/shard_map/ppermute | solution.py:359
  42.2 6.7 %collective-permute-start.11 = (f32[8,128]{1,0:T(8,128)S(1)}, f32[8,128]{1,0:T(8,128)S(1)}, u32[]{:S(2)}, u32[]{:S(2)}) collective-permute-start(f32[8,128]{1,0:T(8,128)S(1)} %merge_rows.1.own_ref.refs_4_), channel_id=1, source_target_pairs={{0,2},{1,5},{2,0},{3,7},{4,6},{5,1},{6,4},{7,3},{8,10},{9,13},{10,... | collective-permute-start | bytes 12296 | tf_op jit(solution)/shard_map/ppermute | solution.py:359
  48.9 0.1 collective-permute-start.10
  49.0 1.5 %collective-permute-done.11.second_ref = f32[8,128]{1,0:T(8,128)S(1)} collective-permute-done((f32[8,128]{1,0:T(8,128)S(1)}, f32[8,128]{1,0:T(8,128)S(1)}, u32[]{:S(2)}, u32[]{:S(2)}) %collective-permute-start.11) | collective-permute-done | bytes 4128 | tf_op jit(solution)/shard_map/ppermute | solution.py:359
  50.5 2.0 %collective-permute-done.10.first_ref = f32[8,128]{1,0:T(8,128)S(1)} collective-permute-done((f32[8,128]{1,0:T(8,128)S(1)}, f32[8,128]{1,0:T(8,128)S(1)}, u32[]{:S(2)}, u32[]{:S(2)}) %collective-permute-start.10) | collective-permute-done | bytes 4128 | tf_op jit(solution)/shard_map/ppermute | solution.py:359
  52.5 1.8 %collective-permute-start.12 = (f32[8,128]{1,0:T(8,128)S(1)}, f32[8,128]{1,0:T(8,128)S(1)}, u32[]{:S(2)}, u32[]{:S(2)}) collective-permute-start(f32[8,128]{1,0:T(8,128)S(1)} %share_rows.1.refs_0_), channel_id=1, source_target_pairs={{0,1},{1,0},{2,3},{3,2},{4,5},{5,4},{6,7},{7,6},{8,9},{9,8},{10,11... | collective-permute-start | bytes 12296 | tf_op jit(solution)/shard_map/ppermute | solution.py:359
  54.3 0.0 copy-done.3
  54.3 0.1 row_weights.1
  54.4 0.7 collective-permute-done.12.refs_1_
  55.1 0.0 copy-done.2
  55.1 19.3 %column_lse.1 = (f32[16,128]{1,0:T(8,128)S(1)}, f32[8,128]{1,0:T(8,128)S(1)}) custom-call(f32[8,128]{1,0:T(8,128)S(1)} %share_rows.1.refs_0_, f32[8,128]{1,0:T(8,128)S(1)} %collective-permute-done.12.refs_1_, f32[256,2048]{1,0:T(8,128)S(1)} %get-tuple-element.56.refs_2_, f32[256,2048]{1,0:T(8,128)S(1)} %get-tuple-element.57.refs_3_, ...), custom_call_target="tpu_custom_call" | custom-call | flops 4194304 | bytes 8388608 | tf_op jit(solution)/shard_map/column_lse/pallas_call | solution.py:297
  74.4 2.0 %collective-permute-start.15 = (f32[16,128]{1,0:T(8,128)S(1)}, f32[16,128]{1,0:T(8,128)S(1)}, u32[]{:S(2)}, u32[]{:S(2)}) collective-permute-start(f32[16,128]{1,0:T(8,128)S(1)} %get-tuple-element.77), channel_id=1, source_target_pairs={{0,24},{8,16},{16,8},{24,0},{1,25},{9,17},{17,9},{25,1},{2,26},{10... | collective-permute-start | bytes 24584 | tf_op jit(solution)/shard_map/ppermute | solution.py:417
  76.4 1.0 %collective-permute-start.14 = (f32[16,128]{1,0:T(8,128)S(1)}, f32[16,128]{1,0:T(8,128)S(1)}, u32[]{:S(2)}, u32[]{:S(2)}) collective-permute-start(f32[16,128]{1,0:T(8,128)S(1)} %get-tuple-element.77), channel_id=1, source_target_pairs={{0,16},{8,24},{16,0},{24,8},{1,17},{9,25},{17,1},{25,9},{2,18},{10... | collective-permute-start | bytes 24584 | tf_op jit(solution)/shard_map/ppermute | solution.py:417
  77.4 0.5 collective-permute-start.13
  77.9 1.1 %treated_pot.1 = f32[8,128]{1,0:T(8,128)} custom-call(f32[8,128]{1,0:T(8,128)S(1)} %get-tuple-element.76.total_ref, bf16[128,1024]{1,0:T(8,128)(2,1)S(1)} %copy-done.2, bf16[128,1024]{1,0:T(8,128)(2,1)S(1)} %collective-permute-done.1.refs_1_.refs_7_, bf16[128,1024]{1,0:T(8,128)(2,1)S(1)} %collective-permute-done.refs_0_.refs_8_.refs_2_, ...), custom_call_target="tpu_custom_call" | custom-call | flops 2097152 | bytes 2097152 | tf_op jit(solution)/shard_map/treated_pot/pallas_call | solution.py:333
  79.0 0.0 collective-permute-done.15
  79.0 1.0 %collective-permute-done.14 = f32[16,128]{1,0:T(8,128)S(1)} collective-permute-done((f32[16,128]{1,0:T(8,128)S(1)}, f32[16,128]{1,0:T(8,128)S(1)}, u32[]{:S(2)}, u32[]{:S(2)}) %collective-permute-start.14) | collective-permute-done | bytes 8224 | tf_op jit(solution)/shard_map/ppermute | solution.py:417
  80.0 1.0 %collective-permute-done.13 = f32[16,128]{1,0:T(8,128)S(1)} collective-permute-done((f32[16,128]{1,0:T(8,128)S(1)}, f32[16,128]{1,0:T(8,128)S(1)}, u32[]{:S(2)}, u32[]{:S(2)}) %collective-permute-start.13) | collective-permute-done | bytes 8224 | tf_op jit(solution)/shard_map/ppermute | solution.py:417
  81.1 0.6 bitcast_subtract_fusion
  (4 shorter events, 0.1 us)
Async XLA Ops:
  0.6 9.2 %copy-start = (bf16[2048,1024]{1,0:T(8,128)(2,1)S(1)}, bf16[2048,1024]{1,0:T(8,128)(2,1)}, u32[]{:S(2)}) copy-start(bf16[2048,1024]{1,0:T(8,128)(2,1)} %refs_20_.1) | copy-start | bytes 12582916
  0.6 6.2 %copy-start.4 = (f32[2048]{0:T(1024)S(1)}, f32[2048]{0:T(1024)}, u32[]{:S(2)}) copy-start(f32[2048]{0:T(1024)} %param.7) | copy-start | bytes 24580
  0.6 9.1 %collective-permute-start.1 = (bf16[128,1024]{1,0:T(8,128)(2,1)}, bf16[128,1024]{1,0:T(8,128)(2,1)S(1)}, u32[]{:S(2)}, u32[]{:S(2)}) collective-permute-start(bf16[128,1024]{1,0:T(8,128)(2,1)} %refs_0_.2), channel_id=1, source_target_pairs={{0,1},{1,0},{2,3},{3,2},{4,5},{5,4},{6,7},{7,6},{8,9},{9,8},{10,11... | collective-permute-start | bytes 786440 | tf_op jit(solution)/shard_map/ppermute | solution.py:359
  1.2 17.5 %collective-permute-start = (bf16[128,1024]{1,0:T(8,128)(2,1)}, bf16[128,1024]{1,0:T(8,128)(2,1)S(1)}, u32[]{:S(2)}, u32[]{:S(2)}) collective-permute-start(bf16[128,1024]{1,0:T(8,128)(2,1)} %refs_0_.2), channel_id=1, source_target_pairs={{0,2},{1,3},{2,4},{3,5},{4,6},{5,7},{6,0},{7,1},{8,10},{9,11},{10,... | collective-permute-start | bytes 786440 | tf_op jit(solution)/shard_map/ppermute | solution.py:359
  7.6 20.6 %collective-permute-start.3 = (bf16[128,1024]{1,0:T(8,128)(2,1)}, bf16[128,1024]{1,0:T(8,128)(2,1)S(1)}, u32[]{:S(2)}, u32[]{:S(2)}) collective-permute-start(bf16[128,1024]{1,0:T(8,128)(2,1)} %refs_0_.2), channel_id=1, source_target_pairs={{0,6},{1,7},{2,0},{3,1},{4,2},{5,3},{6,4},{7,5},{8,14},{9,15},{10,... | collective-permute-start | bytes 786440 | tf_op jit(solution)/shard_map/ppermute | solution.py:359
  9.8 1.0 %copy-start.1 = (bf16[128,1024]{1,0:T(8,128)(2,1)S(1)}, bf16[128,1024]{1,0:T(8,128)(2,1)}, u32[]{:S(2)}) copy-start(bf16[128,1024]{1,0:T(8,128)(2,1)} %refs_0_.2) | copy-start | bytes 786436
  18.7 1.4 %collective-permute-start.4 = (bf16[64,1024]{1,0:T(8,128)(2,1)S(1)}, bf16[64,1024]{1,0:T(8,128)(2,1)S(1)}, u32[]{:S(2)}, u32[]{:S(2)}) collective-permute-start(bf16[64,1024]{1,0:T(8,128)(2,1)S(1)} %get-tuple-element.44), channel_id=1, source_target_pairs={{0,1},{1,0},{2,3},{3,2},{4,5},{5,4},{6,7},{7,6},{8,9},{9,8},{10,11... | collective-permute-start | bytes 393224 | tf_op jit(solution)/shard_map/ppermute | solution.py:359
  18.9 1.4 %collective-permute-start.5 = (bf16[64,1024]{1,0:T(8,128)(2,1)S(1)}, bf16[64,1024]{1,0:T(8,128)(2,1)S(1)}, u32[]{:S(2)}, u32[]{:S(2)}) collective-permute-start(bf16[64,1024]{1,0:T(8,128)(2,1)S(1)} %get-tuple-element.45), channel_id=1, source_target_pairs={{0,1},{1,0},{2,3},{3,2},{4,5},{5,4},{6,7},{7,6},{8,9},{9,8},{10,11... | collective-permute-start | bytes 393224 | tf_op jit(solution)/shard_map/ppermute | solution.py:359
  19.3 18.6 %collective-permute-start.2 = (bf16[128,1024]{1,0:T(8,128)(2,1)S(1)}, bf16[128,1024]{1,0:T(8,128)(2,1)S(1)}, u32[]{:S(2)}, u32[]{:S(2)}) collective-permute-start(bf16[128,1024]{1,0:T(8,128)(2,1)S(1)} %collective-permute-done.refs_0_.refs_8_.refs_2_), channel_id=1, source_target_pairs={{0,2},{1,3},{2,4},{3,5},{4,6},{5,7},{6,0},{7,1},{8,10},{9,11},{10,... | collective-permute-start | bytes 786440 | tf_op jit(solution)/shard_map/ppermute | solution.py:359
  28.2 1.4 %collective-permute-start.6 = (bf16[64,1024]{1,0:T(8,128)(2,1)S(1)}, bf16[64,1024]{1,0:T(8,128)(2,1)S(1)}, u32[]{:S(2)}, u32[]{:S(2)}) collective-permute-start(bf16[64,1024]{1,0:T(8,128)(2,1)S(1)} %get-tuple-element.48), channel_id=1, source_target_pairs={{0,1},{1,0},{2,3},{3,2},{4,5},{5,4},{6,7},{7,6},{8,9},{9,8},{10,11... | collective-permute-start | bytes 393224 | tf_op jit(solution)/shard_map/ppermute | solution.py:359
  28.6 25.7 %copy-start.3 = (f32[1024]{0:T(1024)S(1)}, f32[1024]{0:T(1024)}, u32[]{:S(2)}) copy-start(f32[1024]{0:T(1024)} %param.9) | copy-start | bytes 12292
  28.6 26.5 %copy-start.2 = (bf16[128,1024]{1,0:T(8,128)(2,1)S(1)}, bf16[128,1024]{1,0:T(8,128)(2,1)}, u32[]{:S(2)}) copy-start(bf16[128,1024]{1,0:T(8,128)(2,1)} %refs_0_.2) | copy-start | bytes 786436
  28.6 1.3 %collective-permute-start.7 = (bf16[64,1024]{1,0:T(8,128)(2,1)S(1)}, bf16[64,1024]{1,0:T(8,128)(2,1)S(1)}, u32[]{:S(2)}, u32[]{:S(2)}) collective-permute-start(bf16[64,1024]{1,0:T(8,128)(2,1)S(1)} %get-tuple-element.49), channel_id=1, source_target_pairs={{0,1},{1,0},{2,3},{3,2},{4,5},{5,4},{6,7},{7,6},{8,9},{9,8},{10,11... | collective-permute-start | bytes 393224 | tf_op jit(solution)/shard_map/ppermute | solution.py:359
  37.8 1.6 %collective-permute-start.8 = (bf16[128,1024]{1,0:T(8,128)(2,1)S(1)}, bf16[128,1024]{1,0:T(8,128)(2,1)S(1)}, u32[]{:S(2)}, u32[]{:S(2)}) collective-permute-start(bf16[128,1024]{1,0:T(8,128)(2,1)S(1)} %collective-permute-done.2.refs_0_.refs_14_.refs_8_), channel_id=1, source_target_pairs={{0,1},{1,0},{2,3},{3,2},{4,5},{5,4},{6,7},{7,6},{8,9},{9,8},{10,11... | collective-permute-start | bytes 786440 | tf_op jit(solution)/shard_map/ppermute | solution.py:359
  41.0 1.2 %collective-permute-start.9 = (f32[8,128]{1,0:T(8,128)S(1)}, f32[8,128]{1,0:T(8,128)S(1)}, u32[]{:S(2)}, u32[]{:S(2)}) collective-permute-start(f32[8,128]{1,0:T(8,128)S(1)} %get-tuple-element.55.first_ref), channel_id=1, source_target_pairs={{0,1},{1,0},{2,3},{3,2},{4,5},{5,4},{6,7},{7,6},{8,9},{9,8},{10,11... | collective-permute-start | bytes 12296 | tf_op jit(solution)/shard_map/ppermute | solution.py:359
  42.2 8.2 %collective-permute-start.11 = (f32[8,128]{1,0:T(8,128)S(1)}, f32[8,128]{1,0:T(8,128)S(1)}, u32[]{:S(2)}, u32[]{:S(2)}) collective-permute-start(f32[8,128]{1,0:T(8,128)S(1)} %merge_rows.1.own_ref.refs_4_), channel_id=1, source_target_pairs={{0,2},{1,5},{2,0},{3,7},{4,6},{5,1},{6,4},{7,3},{8,10},{9,13},{10,... | collective-permute-start | bytes 12296 | tf_op jit(solution)/shard_map/ppermute | solution.py:359
  48.9 3.6 %collective-permute-start.10 = (f32[8,128]{1,0:T(8,128)S(1)}, f32[8,128]{1,0:T(8,128)S(1)}, u32[]{:S(2)}, u32[]{:S(2)}) collective-permute-start(f32[8,128]{1,0:T(8,128)S(1)} %merge_rows.1.own_ref.refs_4_), channel_id=1, source_target_pairs={{0,2},{1,7},{2,0},{3,5},{4,6},{5,3},{6,4},{7,1},{8,10},{9,15},{10,... | collective-permute-start | bytes 12296 | tf_op jit(solution)/shard_map/ppermute | solution.py:359
  52.5 2.6 %collective-permute-start.12 = (f32[8,128]{1,0:T(8,128)S(1)}, f32[8,128]{1,0:T(8,128)S(1)}, u32[]{:S(2)}, u32[]{:S(2)}) collective-permute-start(f32[8,128]{1,0:T(8,128)S(1)} %share_rows.1.refs_0_), channel_id=1, source_target_pairs={{0,1},{1,0},{2,3},{3,2},{4,5},{5,4},{6,7},{7,6},{8,9},{9,8},{10,11... | collective-permute-start | bytes 12296 | tf_op jit(solution)/shard_map/ppermute | solution.py:359
  74.4 4.6 %collective-permute-start.15 = (f32[16,128]{1,0:T(8,128)S(1)}, f32[16,128]{1,0:T(8,128)S(1)}, u32[]{:S(2)}, u32[]{:S(2)}) collective-permute-start(f32[16,128]{1,0:T(8,128)S(1)} %get-tuple-element.77), channel_id=1, source_target_pairs={{0,24},{8,16},{16,8},{24,0},{1,25},{9,17},{17,9},{25,1},{2,26},{10... | collective-permute-start | bytes 24584 | tf_op jit(solution)/shard_map/ppermute | solution.py:417
  76.4 3.7 %collective-permute-start.14 = (f32[16,128]{1,0:T(8,128)S(1)}, f32[16,128]{1,0:T(8,128)S(1)}, u32[]{:S(2)}, u32[]{:S(2)}) collective-permute-start(f32[16,128]{1,0:T(8,128)S(1)} %get-tuple-element.77), channel_id=1, source_target_pairs={{0,16},{8,24},{16,0},{24,8},{1,17},{9,25},{17,1},{25,9},{2,18},{10... | collective-permute-start | bytes 24584 | tf_op jit(solution)/shard_map/ppermute | solution.py:417
  77.4 3.7 %collective-permute-start.13 = (f32[16,128]{1,0:T(8,128)S(1)}, f32[16,128]{1,0:T(8,128)S(1)}, u32[]{:S(2)}, u32[]{:S(2)}) collective-permute-start(f32[16,128]{1,0:T(8,128)S(1)} %get-tuple-element.77), channel_id=1, source_target_pairs={{0,8},{8,0},{16,24},{24,16},{1,9},{9,1},{17,25},{25,17},{2,10},{10... | collective-permute-start | bytes 24584 | tf_op jit(solution)/shard_map/ppermute | solution.py:417
